TPU v7x, 32 devices: a whole 2x2x4 slice. The times are simulated.
32 devices in a mesh: gx: 8 (over y, x, core), gy: 4 (over z).
Axes of the slice: x: 2, y: 2, z: 4, core: 2. Of those that a mesh axis runs over, the one named last changes fastest.
Arguments:
- tokens: bfloat16 [16384, 1536], P(('gx', 'gy')), may hold values from -6 to 6
- attn_gain: float32 [1536], replicated, may hold values from 0.25 to 1.75
- query_key_value_weight: bfloat16 [1536, 2560], P('gx', 'gy'), may hold values from -0.15625 to 0.15625
- out_weight: bfloat16 [1536, 1536], P('gy', 'gx'), may hold values from -0.875 to 0.875
- moe_gain: float32 [1536], replicated, may hold values from 0.25 to 1.75
- router_weight: bfloat16 [40, 1536], P('gy', 'gx'), may hold values from -0.078125 to 0.078125
- expert_in: bfloat16 [40, 1536, 1024], P('gy', 'gx'), may hold values from -0.15625 to 0.15625
- expert_out: bfloat16 [40, 1536, 512], P('gy', 'gx'), may hold values from -0.75 to 0.75
- expert_ids: int32 [16384, 8], P('gx'), may hold values from 0 to 39, all different within a row
- route_order: int32 [8, 16384], P('gx'), may hold values from 0 to 16383, each once within a row
- segment_ids: int32 [8, 2048], P('gx'), may hold values from 0 to 15, never falling along the last dimension, each value on 1 to 256 neighbouring positions
- out_grad: bfloat16 [16384, 1536], P(('gx', 'gy')), may hold values from -6 to 6
Outputs:
- layer_out: bfloat16 [16384, 1536], P(('gx', 'gy'))
- input_grad: float32 [16384, 1536], P(('gx', 'gy'))
- attn_gain_grad: float32 [1536], replicated
- qkv_grad: float32 [1536, 2560], P('gx', 'gy')
- out_weight_grad: float32 [1536, 1536], P('gy', 'gx')
- moe_gain_grad: float32 [1536], replicated
- router_grad: float32 [40, 1536], P('gy', 'gx')
- expert_in_grad: float32 [40, 1536, 1024], P('gy', 'gx')
- expert_out_grad: float32 [40, 1536, 512], P('gy', 'gx')
Inputs may be any that keep to these rules, and one draw needn't show every extreme that they name: `expert_ids`: the 8 experts of a token differ from one another. `route_order`: each row holds every number of 0 to 16383 once; entry t * 8 + k is the rank of the k-th choice of the sequence's token t. `segment_ids`: document numbers never fall along a row; a document holds at most 256 positions.
All inputs are finite; a program needn't handle non-finite values.
Results may differ from a plain program's by a relative error of at most 0.02.
Values may be sent and summed in bfloat16 or wider, within the bound.
No kernel may reach another device: no remote copies, remote signals or barrier semaphores. Data moves between devices by JAX's collectives and lax.ppermute only.
A program may use at most 320 MiB of HBM per device.

v0:
```python
import functools

import jax
import jax.numpy as jnp
from jax import lax
from jax.experimental import pallas as pl
from jax.experimental.pallas import tpu as pltpu
from jax.sharding import PartitionSpec as P

D = 1536
HEAD_WIDTH = 64
FF = 512
TOPK = 8
SEGMAX = 256
QUERIES_PER_GROUP = 3
CAP = 460
SLOTS = 464
WINDOW = 128
SHORT_WINDOW = 96
CHUNK = 256
LANES = 128
SUBLANES = 16

EPS = 1e-05
MASKED = -1e30
SCORE_SCALE = HEAD_WIDTH ** (-0.5)
VMEM_BYTES = 60 * 1024 * 1024
F32 = jnp.float32
BF16 = jnp.bfloat16


def dot_nn(a, b):
    return lax.dot_general(a, b, (((1,), (0,)), ((), ())), preferred_element_type=F32)


def dot_nt(a, b):
    return lax.dot_general(a, b, (((1,), (1,)), ((), ())), preferred_element_type=F32)


def dot_tn(a, b):
    return lax.dot_general(a, b, (((0,), (0,)), ((), ())), preferred_element_type=F32)


def params(**more):
    return pltpu.CompilerParams(vmem_limit_bytes=VMEM_BYTES, **more)


def cost(micros):
    return pl.CostEstimate(
        flops=int(micros * 1.1e9), bytes_accessed=int(micros * 3.6e6), transcendentals=0
    )


def store_halves(half_ref, mine_ref, other_ref, columns, value):
    slices, depth, _ = mine_ref.shape
    for parity in range(2):
        own = half_ref[0] == parity
        for ref, taken in ((mine_ref, own), (other_ref, jnp.logical_not(own))):

            @pl.when(taken)
            def _(ref=ref, parity=parity):
                for n in range(slices):
                    at = (2 * n + parity) * depth
                    ref[n, :, columns] = value[at : at + depth]


def whole(shape):
    return pl.BlockSpec(shape, lambda *_: (0,) * len(shape))


def once(shape):
    return pl.BlockSpec(shape, lambda *_: (0,) * len(shape), pipeline_mode=pl.Buffered(1))


def rope_tiles(first_row, rows):
    half = HEAD_WIDTH // 2
    freq = jnp.exp(jnp.arange(half, dtype=F32) * (-2.0 * jnp.log(10000.0) / HEAD_WIDTH))
    position = (first_row + jnp.arange(rows, dtype=jnp.int32)).astype(F32)
    angle = position[:, None] * freq[None, :]
    cosine, sine = jnp.cos(angle), jnp.sin(angle)
    return (
        jnp.concatenate([cosine] * 4, axis=1),
        jnp.concatenate([-sine, sine, -sine, sine], axis=1),
    )


def swap_halves(tile):
    lane = lax.broadcasted_iota(jnp.int32, tile.shape, 1)
    half = HEAD_WIDTH // 2
    return jnp.where(
        lane % HEAD_WIDTH < half,
        pltpu.roll(tile, LANES - half, axis=1),
        pltpu.roll(tile, half, axis=1),
    )


def rotate_tile(tile, cosine, sine, sign):
    return tile * cosine + sign * swap_halves(tile) * sine


def key_tables(cosine, sine):
    lane = lax.broadcasted_iota(jnp.int32, cosine.shape, 1)
    is_key = lane < HEAD_WIDTH
    return jnp.where(is_key, cosine, 1.0), jnp.where(is_key, sine, 0.0)


def hold_weight(first_ref, rest_ref, held_ref):
    @pl.when(pl.program_id(0) == 0)
    def _():
        held_ref[...] = first_ref[...].reshape(held_ref.shape)

    @pl.when(pl.program_id(0) > 0)
    def _():
        held_ref[...] = rest_ref[...].reshape(held_ref.shape)


def project_kernel(
    normed_ref, first_ref, rest_ref, cos_ref, sin_ref, query_ref, kv_ref, held_ref
):
    hold_weight(first_ref, rest_ref, held_ref)
    project = dot_nn(normed_ref[...], held_ref[...])
    cosine, sine = cos_ref[...], sin_ref[...]
    key_cos, key_sin = key_tables(cosine, sine)
    for col in range(0, query_ref.shape[1], LANES):
        tile = rotate_tile(project[:, col : col + LANES], cosine, sine, 1.0)
        query_ref[:, col : col + LANES] = tile.astype(BF16)
    for col in range(0, kv_ref.shape[1], LANES):
        at = query_ref.shape[1] + col
        tile = rotate_tile(project[:, at : at + LANES], key_cos, key_sin, 1.0)
        kv_ref[:, col : col + LANES] = tile.astype(BF16)


def group_windows(before, own, group):
    col = group * 2 * HEAD_WIDTH
    return [
        jnp.concatenate([before[:, at : at + HEAD_WIDTH], own[:, at : at + HEAD_WIDTH]], axis=0)
        for at in (col, col + HEAD_WIDTH)
    ]


def stack_heads(block, group):
    at = group * QUERIES_PER_GROUP * HEAD_WIDTH
    return jnp.concatenate(
        [
            block[:, at + i * HEAD_WIDTH : at + (i + 1) * HEAD_WIDTH]
            for i in range(QUERIES_PER_GROUP)
        ],
        axis=0,
    )


def store_heads(ref, group, value_t):
    at = group * QUERIES_PER_GROUP * HEAD_WIDTH
    for i in range(QUERIES_PER_GROUP):
        part = value_t[:, i * SEGMAX : (i + 1) * SEGMAX].T
        ref[:, at + i * HEAD_WIDTH : at + (i + 1) * HEAD_WIDTH] = part.astype(ref.dtype)


def clear_spare(ref, groups):
    used = groups * QUERIES_PER_GROUP * HEAD_WIDTH
    if used < ref.shape[1]:
        ref[:, used:] = jnp.zeros((ref.shape[0], ref.shape[1] - used), ref.dtype)


def probs_of(keys, queries, bias):
    scores = dot_nt(keys, queries) * SCORE_SCALE
    scores = scores + jnp.concatenate([bias] * QUERIES_PER_GROUP, axis=1)
    top = jnp.max(scores, axis=0, keepdims=True)
    weights = jnp.exp(scores - top)
    total = jnp.sum(weights, axis=0, keepdims=True)
    return weights * (1.0 / total)


def attend_kernel(query_ref, own_ref, before_ref, bias_ref, mixed_ref):
    groups = own_ref.shape[1] // (2 * HEAD_WIDTH)
    query, own, before, bias = query_ref[...], own_ref[...], before_ref[...], bias_ref[...]
    clear_spare(mixed_ref, groups)
    for group in range(groups):
        keys, values = group_windows(before, own, group)
        probs = probs_of(keys, stack_heads(query, group), bias).astype(BF16)
        store_heads(mixed_ref, group, dot_nn(values.T, probs))


def attend_back_kernel(
    query_ref, own_ref, before_ref, bias_ref, first_ref, rest_ref, branch_ref, cos_ref, sin_ref,
    dquery_ref, down_ref, dbefore_ref, raw_ref, held_ref,
):
    groups = own_ref.shape[1] // (2 * HEAD_WIDTH)
    hold_weight(first_ref, rest_ref, held_ref)
    mixed_grad = dot_nn(branch_ref[...], held_ref[...]).astype(BF16)
    query, own, before, bias = query_ref[...], own_ref[...], before_ref[...], bias_ref[...]
    clear_spare(raw_ref, groups)
    for group in range(groups):
        keys, values = group_windows(before, own, group)
        queries, grads = stack_heads(query, group), stack_heads(mixed_grad, group)
        probs = probs_of(keys, queries, bias)
        prob_grad = dot_nt(values, grads)
        inner = jnp.sum(probs * prob_grad, axis=0, keepdims=True)
        score_grad = (SCORE_SCALE * probs * (prob_grad - inner)).astype(BF16)
        store_heads(raw_ref, group, dot_nn(keys.T, score_grad))
        col = group * 2 * HEAD_WIDTH
        for at, part in (
            (col, dot_nn(score_grad, queries)),
            (col + HEAD_WIDTH, dot_nn(probs.astype(BF16), grads)),
        ):
            dbefore_ref[:, at : at + HEAD_WIDTH] = part[:SEGMAX].astype(dbefore_ref.dtype)
            down_ref[:, at : at + HEAD_WIDTH] = part[SEGMAX:]
    cosine, sine = cos_ref[...], sin_ref[...]
    for col in range(0, query_ref.shape[1], LANES):
        tile = rotate_tile(raw_ref[:, col : col + LANES], cosine, sine, -1.0)
        dquery_ref[:, col : col + LANES] = tile.astype(BF16)


def branch_weights_kernel(experts, halves, normed_t_ref, *refs):
    branch_refs, refs = refs[:halves], refs[halves:]
    high_refs, low_refs, refs = refs[:halves], refs[halves : 2 * halves], refs[2 * halves :]
    *mixed_refs, term_ref, turned_ref, router_ref = refs
    block = pl.program_id(0)
    width = mixed_refs[0].shape[1]

    @pl.when(block == 0)
    def _():
        turned_ref[...] = jnp.concatenate([ref[...].T for ref in branch_refs], axis=1)
        high, low = (
            jnp.concatenate([ref[...] for ref in part], axis=0) for part in (high_refs, low_refs)
        )
        normed_t = normed_t_ref[...]
        router_ref[...] = dot_nn(normed_t, high) + dot_nn(normed_t, low)

    mixed = jnp.concatenate([ref[...] for ref in mixed_refs], axis=0)
    out_grad = dot_nn(turned_ref[...], mixed).astype(BF16)
    slices, depth, _ = term_ref.shape
    term_ref[:, :, :width] = out_grad.reshape(slices, depth, width)
    router = pltpu.roll(router_ref[...], (LANES - block * experts) % LANES, axis=1)
    term_ref[:, :, width:] = router.astype(BF16).reshape(slices, depth, LANES)


def branch_kernel(halves, *refs):
    mixed_refs = refs[:halves]
    first_ref, rest_ref, inputs_ref, gain_ref, middle_ref, *normed_refs = refs[halves:]
    width = first_ref.shape[-1]
    blocks = [first_ref[...].reshape(D, width)]
    blocks += [rest_ref[:, n].reshape(D, width) for n in range(rest_ref.shape[1])]
    weight = jnp.concatenate(blocks, axis=1)
    mixed = jnp.concatenate([ref[...] for ref in mixed_refs], axis=0)
    middle = inputs_ref[...].astype(F32) + dot_nt(mixed, weight)
    scale = lax.rsqrt(jnp.mean(middle * middle, axis=1, keepdims=True) + EPS)
    middle_ref[...] = middle
    normed = (middle * scale * gain_ref[...]).astype(BF16)
    for n, ref in enumerate(normed_refs):
        ref[...] = normed[n * CHUNK : (n + 1) * CHUNK]


def middle_back_kernel(
    own_ref, up_ref, down_ref, gates_ref, select_ref, router_ref, middle_ref, gain_ref, grad_ref,
    middle_grad_ref, branch_ref, high_ref, low_ref, gain_grad_ref,
):
    grad = own_ref[...].astype(F32) + up_ref[...].astype(F32) + down_ref[...].astype(F32)
    pairs = dot_nn(grad[:, D:].astype(BF16), select_ref[...])
    gates, router = gates_ref[...], router_ref[...]
    logit_grad = gates * (pairs - jnp.sum(gates * pairs, axis=1, keepdims=True))
    high = logit_grad.astype(BF16)
    low = (logit_grad - high.astype(F32)).astype(BF16)
    high_ref[...] = high
    low_ref[...] = low
    grad = grad[:, :D] + dot_nt(high, router) + dot_nt(low, router)
    back, gain_grad = norm_back(middle_ref[...], gain_ref[...], grad)
    middle_grad = grad_ref[...].astype(F32) + back
    middle_grad_ref[...] = middle_grad
    branch_ref[...] = middle_grad.astype(BF16)

    @pl.when(pl.program_id(0) == 0)
    def _():
        gain_grad_ref[...] = gain_grad

    @pl.when(pl.program_id(0) > 0)
    def _():
        gain_grad_ref[...] += gain_grad


def project_back_kernel(halves, *refs):
    dquery_refs, refs = refs[:halves], refs[halves:]
    own_refs, refs = refs[:halves], refs[halves:]
    next_refs, refs = refs[:halves], refs[halves:]
    (half_ref, normed_t_ref, first_ref, rest_ref, cos_ref, sin_ref, mine_ref, other_ref, total_ref,
     held_ref) = refs
    block = pl.program_id(0)
    key_cos, key_sin = key_tables(cos_ref[...], sin_ref[...])
    tiles = [jnp.concatenate([ref[...] for ref in dquery_refs], axis=0)]
    for col in range(0, own_refs[0].shape[1], LANES):
        cols = slice(col, col + LANES)
        tile = jnp.concatenate(
            [own[:, cols] + after_[:, cols].astype(F32) for own, after_ in zip(own_refs, next_refs)],
            axis=0,
        )
        tiles.append(rotate_tile(tile, key_cos, key_sin, -1.0).astype(BF16))
    grads = jnp.concatenate(tiles, axis=1)
    hold_weight(first_ref, rest_ref, held_ref)
    dweight = dot_nn(normed_t_ref[...], grads).astype(BF16)
    store_halves(half_ref, mine_ref, other_ref, slice(0, grads.shape[1]), dweight)
    part = dot_nt(grads, held_ref[...])

    @pl.when(block == 0)
    def _():
        total_ref[...] = part

    @pl.when(block > 0)
    def _():
        total_ref[...] += part


def input_back_kernel(
    inputs_ref, total_ref, gain_ref, middle_grad_ref, input_grad_ref, gain_grad_ref
):
    back, gain_grad = norm_back(inputs_ref[...].astype(F32), gain_ref[...], total_ref[...])
    input_grad_ref[...] = middle_grad_ref[...] + back

    @pl.when(pl.program_id(0) == 0)
    def _():
        gain_grad_ref[...] = gain_grad

    @pl.when(pl.program_id(0) > 0)
    def _():
        gain_grad_ref[...] += gain_grad


def joined_sum_kernel(groups, *refs):
    *part_refs, out_ref = refs
    rows = out_ref.shape[0]
    total = part_refs[0][...].astype(F32)
    for ref in part_refs[1:]:
        total = total + ref[:rows, :].astype(F32)
    queries = QUERIES_PER_GROUP * HEAD_WIDTH
    span = queries + 2 * HEAD_WIDTH
    width = total.shape[1] - groups * 2 * HEAD_WIDTH
    for group in range(groups):
        at = group * span
        out_ref[:, at : at + queries] = total[:, group * queries : (group + 1) * queries]
        col = width + group * 2 * HEAD_WIDTH
        out_ref[:, at + queries : at + span] = total[:, col : col + 2 * HEAD_WIDTH]


def norm_back(resid, gain, grad):
    scale = lax.rsqrt(jnp.mean(resid * resid, axis=1, keepdims=True) + EPS)
    gain_grad = jnp.sum(grad * resid * scale, axis=0, keepdims=True)
    scaled = grad * gain
    inner = jnp.sum(scaled * resid, axis=1, keepdims=True)
    return scale * scaled - resid * (scale * scale * scale * inner / D), gain_grad


def slots_kernel(experts, first_ref, ids_ref, rank_ref, pos_ref, ends_ref):
    length = ids_ref.shape[1]
    row = lax.broadcasted_iota(jnp.int32, (SUBLANES, length), 0)
    wanted = jnp.where(row < experts, row + first_ref[0], -1)
    rank = jnp.full((SUBLANES, length), 1 << 30, jnp.int32)
    for k in range(TOPK):
        rank = jnp.where(ids_ref[k : k + 1, :] == wanted, rank_ref[k : k + 1, :], rank)
    limit = jnp.zeros((SUBLANES, 1), jnp.int32)
    for bit in reversed(range((length * TOPK).bit_length())):
        higher = limit + (1 << bit)
        count = jnp.sum(jnp.where(rank < higher, 1.0, 0.0), axis=1, keepdims=True)
        limit = jnp.where(count <= CAP, higher, limit)
    kept = jnp.where(rank < limit, 1.0, 0.0)
    before = jnp.where(
        lax.broadcasted_iota(jnp.int32, (CHUNK, CHUNK), 0)
        < lax.broadcasted_iota(jnp.int32, (CHUNK, CHUNK), 1),
        1.0,
        0.0,
    ).astype(BF16)
    lane = lax.broadcasted_iota(jnp.int32, ends_ref.shape, 1)
    so_far = jnp.zeros((SUBLANES, 1), F32)
    ends = jnp.zeros(ends_ref.shape, F32)
    for n in range(length // CHUNK):
        part = kept[:, n * CHUNK : (n + 1) * CHUNK]
        place = dot_nn(part.astype(BF16), before) + so_far
        pos_ref[n] = jnp.where(part > 0.5, place, -1.0).astype(jnp.int32)
        so_far = so_far + jnp.sum(part, axis=1, keepdims=True)
        ends = jnp.where(lane == n + 1, so_far, ends)
    ends_ref[...] = ends.astype(jnp.int32)


def slot_windows(ends_ref, experts, chunk, window):
    firsts = [ends_ref[e, chunk] // SUBLANES * SUBLANES for e in range(experts)]
    ends = [ends_ref[e, chunk + 1] for e in range(experts)]
    count = jnp.int32(0)
    for first, end in zip(firsts, ends):
        count = jnp.maximum(count, (end - first + window - 1) // window)
    return firsts, ends, count


def window_start(first, n_window, window):
    return pl.multiple_of(jnp.minimum(first + n_window * window, SLOTS - window), SUBLANES)


def dispatch_kernel(with_gates, experts, size, *refs):
    shard_ref, ends_ref, *refs = refs
    if with_gates:
        *x_refs, pos_ref, router_ref, member_ref, out_ref, gate_ref, hot_ref, held_ref, sems = refs
    else:
        *x_refs, pos_ref, out_ref, hot_ref, held_ref, sems = refs
    window = hot_ref.shape[0] // experts
    span = 2 * size - 1
    parts = len(x_refs) // span
    part_rows = held_ref.shape[1] // parts

    def fetch(n, part, source):
        rows = pl.ds(part * part_rows, part_rows)
        return pltpu.make_async_copy(
            x_refs[part * span + source], held_ref.at[n, rows, :], sems.at[n, part]
        )

    for n in range(size):
        for part in range(parts):
            if n == 0:
                fetch(n, part, 0).start()
            else:
                below = shard_ref[0] >= n

                @pl.when(below)
                def _(n=n, part=part):
                    fetch(n, part, n).start()

                @pl.when(jnp.logical_not(below))
                def _(n=n, part=part):
                    fetch(n, part, span - n).start()

    out_ref[...] = jnp.zeros(out_ref.shape, BF16)
    if with_gates:
        gate_ref[...] = jnp.zeros(gate_ref.shape, F32)
    row = lax.broadcasted_iota(jnp.int32, (window, CHUNK), 0)
    halves = held_ref.shape[1] // CHUNK
    for n in range(size):
        for part in range(parts):
            fetch(n, part, 0).wait()
        for half in range(halves):
            chunk = shard_ref[n] * halves + half
            x = held_ref[n, half * CHUNK : (half + 1) * CHUNK, :]
            pos = pos_ref[chunk]
            firsts, ends, count = slot_windows(ends_ref, experts, chunk, window)
            if with_gates:
                logits = jnp.where(member_ref[chunk] > 0.5, dot_nn(x, router_ref[...]), MASKED)
                raised = jnp.exp(logits)
                gates = raised / jnp.sum(raised, axis=1, keepdims=True)
                lane = lax.broadcasted_iota(jnp.int32, gates.shape, 1)
                gates = jnp.where(lane < SUBLANES, gates, 0.0)
                high = gates.astype(BF16).astype(F32)
                gates = (high + pltpu.roll(gates - high, SUBLANES, axis=1)).astype(BF16)

            def body(n_window, _):
                for e in range(experts):
                    start = firsts[e] + n_window * window
                    at = window_start(firsts[e], n_window, window)
                    place = pos[e : e + 1, :]
                    place = jnp.where(place >= start, place - at, -1)
                    hot_ref[e * window : (e + 1) * window, :] = jnp.where(
                        row == place, 1.0, 0.0
                    ).astype(BF16)
                hot = hot_ref[...]
                rows = dot_nn(hot, x)
                if with_gates:
                    gate_rows = dot_nn(hot, gates)
                for e in range(experts):
                    start = firsts[e] + n_window * window
                    at = window_start(firsts[e], n_window, window)
                    part = slice(e * window, (e + 1) * window)

                    @pl.when(start < ends[e])
                    def _():
                        out_ref[e, pl.ds(at, window), :] += rows[part].astype(BF16)
                        if with_gates:
                            gate_ref[e, pl.ds(at, window), :] += gate_rows[part]

                return 0

            lax.fori_loop(0, count, body, 0)


def combine_kernel(with_pairs, sizes, order, *refs):
    piece_ref, ends_ref, place_ref, *refs = refs
    rows_refs, refs = refs[: len(sizes)], refs[len(sizes) :]
    if with_pairs:
        pair_refs, refs = refs[: len(sizes)], refs[len(sizes) :]
        *out_refs, held_ref, sems, hot_ref, total_ref, held_pair_ref, pair_total_ref = refs
    else:
        *out_refs, held_ref, sems, hot_ref, total_ref = refs
    experts = sum(sizes)
    count_out = len(out_refs)
    home = [(n, e) for n, size in enumerate(sizes) for e in range(size)]
    step, steps = pl.program_id(0), pl.num_programs(0)
    halves = steps // len(order)
    visits = steps // count_out

    def chunk_of(at_step):
        return piece_ref[at_step // halves] * halves + at_step % halves

    def copies(chunk, n_window, slot):
        firsts = slot_windows(ends_ref, experts, chunk, WINDOW)[0]
        return [
            pltpu.make_async_copy(
                rows_refs[n].at[own, pl.ds(window_start(firsts[e], n_window, WINDOW), WINDOW), :],
                held_ref.at[slot, pl.ds(e * WINDOW, WINDOW), :],
                sems.at[slot, e],
            )
            for e, (n, own) in enumerate(home)
        ]

    @pl.when(step == 0)
    def _():
        for copy in copies(chunk_of(step), 0, 0):
            copy.start()

    @pl.when(step + 1 < steps)
    def _():
        for copy in copies(chunk_of(step + 1), 0, (step + 1) % 2):
            copy.start()

    chunk = chunk_of(step)
    firsts, ends, count = slot_windows(ends_ref, experts, chunk, WINDOW)
    lane = lax.broadcasted_iota(jnp.int32, (CHUNK, WINDOW), 1)
    places = place_ref[...]

    def mark(n_window):
        for e, (n, own) in enumerate(home):
            start = firsts[e] + n_window * WINDOW
            at = window_start(firsts[e], n_window, WINDOW)
            place = places[:, e : e + 1]
            place = jnp.where(place >= start, place - at, -1)
            cols = slice(e * WINDOW, (e + 1) * WINDOW)
            hot_ref[:, cols] = jnp.where(lane == place, 1.0, 0.0).astype(BF16)
            if with_pairs:
                held_pair_ref[cols, :] = pair_refs[n][own, pl.ds(at, WINDOW), :]

    mark(0)
    for copy in copies(chunk, 0, step % 2):
        copy.wait()
    total_ref[...] = dot_nn(hot_ref[...], held_ref[step % 2])
    if with_pairs:
        pair_total_ref[...] = dot_nn(hot_ref[...], held_pair_ref[...])

    def body(n_window, _):
        more = copies(chunk, n_window, 2)
        for copy in more:
            copy.start()
        mark(n_window)
        for copy in more:
            copy.wait()
        total_ref[...] += dot_nn(hot_ref[...], held_ref[2])
        if with_pairs:
            pair_total_ref[...] += dot_nn(hot_ref[...], held_pair_ref[...])
        return 0

    lax.fori_loop(1, count, body, 0)
    for n, out_ref in enumerate(out_refs):

        @pl.when(step // visits == n)
        def _(n=n * visits // halves, out_ref=out_ref):
            out_ref[:, :D] = total_ref[...].astype(BF16)
            if with_pairs:
                place = -order[n] % len(order) * 2 * experts
                out_ref[:, D:] = pltpu.roll(pair_total_ref[...], place, axis=1).astype(BF16)


def expert_kernel(
    first, experts, half_ref, x_ref, grad_ref, gate_ref, weight_ref, y_ref, z_ref, pair_ref, *term_refs,
):
    e = first + pl.program_id(0)
    x, slot_grad = x_ref[0], grad_ref[0]
    w_in, w_out = weight_ref[0, :, : 2 * FF], weight_ref[0, :, 2 * FF :]
    lane = lax.broadcasted_iota(jnp.int32, gate_ref.shape[1:], 1)
    gate = jnp.sum(
        jnp.where((lane == e) | (lane == e + SUBLANES), gate_ref[0], 0.0), axis=1, keepdims=True
    )
    gate_up = dot_nn(x, w_in)
    gate_part, up_part = gate_up[:, :FF], gate_up[:, FF:]
    sigmoid = jax.nn.sigmoid(gate_part)
    silu = gate_part * sigmoid
    hidden = (silu * up_part).astype(BF16)
    raw = dot_nn(slot_grad, w_out)
    pair = jnp.sum(hidden.astype(F32) * raw, axis=1, keepdims=True)
    high = pair.astype(BF16).astype(F32)
    pair_ref[0] = jnp.where(
        lane == e, high, jnp.where(lane == e + experts, pair - high, 0.0)
    ).astype(BF16)
    hidden_grad = gate * raw
    gate_up_grad = jnp.concatenate(
        [
            (hidden_grad * up_part * sigmoid * (1.0 + gate_part * (1.0 - sigmoid))).astype(BF16),
            (hidden_grad * silu).astype(BF16),
        ],
        axis=1,
    )
    z_ref[0] = dot_nt(gate_up_grad, w_in).astype(BF16)
    y_ref[0] = (gate * dot_nt(hidden, w_out)).astype(BF16)
    rows_grad = (gate * slot_grad.astype(F32)).astype(BF16)
    in_term = dot_tn(x, gate_up_grad).astype(BF16)
    out_term = dot_tn(rows_grad, hidden).astype(BF16)
    if len(term_refs) == 2:
        store_halves(half_ref, *term_refs, slice(0, 2 * FF), in_term)
        store_halves(half_ref, *term_refs, slice(2 * FF, 3 * FF), out_term)
    else:
        term_ref = term_refs[0]
        slices, depth, _ = term_ref.shape
        term_ref[:, :, : 2 * FF] = in_term.reshape(slices, depth, 2 * FF)
        term_ref[:, :, 2 * FF :] = out_term.reshape(slices, depth, FF)


def after(value, *others):
    return lax.optimization_barrier((value,) + others)[0]


def pair_scatter(mine, other, size, *gates):
    taken = after(lax.ppermute(other, "gx", [(s, s ^ 1) for s in range(size)]), *gates)
    mine = (mine.astype(F32) + taken.astype(F32)).astype(mine.dtype)
    groups = [list(range(0, size, 2)), list(range(1, size, 2))]
    total = lax.psum_scatter(mine, "gx", scatter_dimension=0, tiled=True, axis_index_groups=groups)
    return lax.optimization_barrier(total)[0]


def direct_gather(part, size):
    return jnp.stack(
        [
            lax.ppermute(part, "gy", [(s, (s + k) % size) for s in range(size)])
            for k in range(1, size)
        ]
    )


def gather_step(pair, step, size, *gates):
    up, down = (after(part, *gates) if gates else part for part in pair)
    return (
        lax.ppermute(up, "gy", [(s, s + 1) for s in range(step, size - 1)]),
        lax.ppermute(down, "gy", [(s + 1, s) for s in range(0, size - 1 - step)]),
    )


def sum_added(parts, pair, step, size, *gates):
    above, below = parts[step], parts[size - step]
    if gates:
        pair = tuple(after(part, *gates) for part in pair)
    if pair is not None:
        above, below = (
            (a.astype(F32) + b.astype(F32)).astype(a.dtype)
            for a, b in zip((above, below), pair)
        )
    return above, below


def sum_sent(added, step, size):
    above, below = added
    return (
        lax.ppermute(above, "gy", [(s, s + 1) for s in range(step)]),
        lax.ppermute(below, "gy", [(size - 1 - s, size - 2 - s) for s in range(step)]),
    )


def sum_step(parts, pair, step, size, *gates):
    return sum_sent(sum_added(parts, pair, step, size, *gates), step, size)


def sum_steps_of(parts, size, gates):
    steps, pair = [], None
    for step in range(1, size):
        pair = sum_step(parts, pair, step, size, *gates.get(step, ()))
        steps.append(pair)
    return steps


def direct_sum(parts, size, *gates):
    taken = [
        lax.ppermute(parts[k], "gy", [(s, (s - k) % size) for s in range(size)])
        for k in range(1, size)
    ]
    total = parts[0].astype(F32)
    for part in taken:
        total = total + after(part, *gates).astype(F32)
    return total


def summed(parts, steps):
    return parts[0].astype(F32) + steps[-1][0].astype(F32) + steps[-1][1].astype(F32)


def shards(
    nx,
    ny,
    tokens,
    attn_gain,
    query_key_value_weight,
    out_weight,
    moe_gain,
    router_weight,
    expert_in,
    expert_out,
    expert_ids,
    route_order,
    segment_ids,
    out_grad,
):
    rows = tokens.shape[0]
    length = segment_ids.shape[1]
    depth = out_weight.shape[1]
    heads_width = out_weight.shape[0]
    groups = heads_width // (HEAD_WIDTH * QUERIES_PER_GROUP)
    spare = -heads_width % LANES
    width = heads_width + spare
    kv_width = groups * 2 * HEAD_WIDTH
    joined = width + kv_width
    experts = router_weight.shape[0]
    all_experts = experts * ny
    chunks = length // CHUNK
    own_chunks = rows // CHUNK
    me = lax.axis_index("gy")
    first_expert = me * experts
    first_row = me * rows
    both = ("gx", "gy")

    pos, ends = pl.pallas_call(
        functools.partial(slots_kernel, experts),
        in_specs=[
            pl.BlockSpec(memory_space=pltpu.SMEM),
            pl.BlockSpec(memory_space=pltpu.VMEM),
            pl.BlockSpec(memory_space=pltpu.VMEM),
        ],
        out_shape=[
            jax.ShapeDtypeStruct((chunks, SUBLANES, CHUNK), jnp.int32),
            jax.ShapeDtypeStruct((SUBLANES, LANES), jnp.int32),
        ],
        compiler_params=params(),
        cost_estimate=cost(3),
        name="slots",
    )(
        first_expert.reshape(1),
        expert_ids.T,
        route_order[0].reshape(length, TOPK).T,
    )
    places = jnp.pad(
        pos.transpose(0, 2, 1).reshape(length, SUBLANES), ((0, 0), (0, LANES - SUBLANES))
    )
    ends = ends[:, : chunks + 1]
    pieces = (me - jnp.arange(ny, dtype=jnp.int32)) % ny
    lane_expert = jnp.arange(LANES, dtype=jnp.int32)
    turned_expert = (me - lane_expert // experts) % ny * experts + lane_expert % experts
    turned_expert = jnp.where(lane_expert < all_experts, turned_expert, -1)
    members = jnp.any(expert_ids[:, :, None] == turned_expert[None, None, :], axis=1)
    members = members.astype(F32).reshape(chunks, CHUNK, LANES)
    own_ids = lax.dynamic_slice_in_dim(expert_ids, first_row, rows, 0)
    own_members = jnp.any(own_ids[:, :, None] == turned_expert[None, None, :], axis=1).astype(F32)

    inputs = tokens.astype(F32)
    scale_one = lax.rsqrt(jnp.mean(inputs * inputs, axis=1, keepdims=True) + EPS)
    normed_one = (inputs * scale_one * attn_gain[None, :]).astype(BF16)
    normed_one_t = normed_one.T
    cosine, sine = rope_tiles(first_row, rows)
    labels = jnp.concatenate([jnp.full((SEGMAX,), -1, jnp.int32), segment_ids[0]])
    labels = lax.dynamic_slice_in_dim(labels, first_row, rows + SEGMAX, 0)
    position = jnp.arange(rows + SEGMAX, dtype=jnp.int32)
    bias = jnp.stack(
        [
            jnp.where(
                (labels[s : s + 2 * SEGMAX, None] == labels[None, s + SEGMAX : s + 2 * SEGMAX])
                & (
                    position[s : s + 2 * SEGMAX, None]
                    <= position[None, s + SEGMAX : s + 2 * SEGMAX]
                ),
                0.0,
                MASKED,
            ).astype(F32)
            for s in range(0, rows, SEGMAX)
        ]
    )
    grouped = query_key_value_weight.reshape(depth, groups, QUERIES_PER_GROUP + 2, HEAD_WIDTH)
    own_joined = jnp.concatenate(
        [
            jnp.pad(
                grouped[:, :, :QUERIES_PER_GROUP].reshape(depth, heads_width), ((0, 0), (0, spare))
            ),
            grouped[:, :, QUERIES_PER_GROUP:].reshape(depth, kv_width),
        ],
        axis=1,
    )
    own_out = jnp.pad(out_weight.T, ((0, 0), (0, spare)))
    own_router = jnp.pad(router_weight.T, ((0, 0), (0, LANES - experts)))
    gap = -(joined + LANES) % width
    own_weights = jnp.concatenate(
        [own_joined, own_router, jnp.zeros((depth, gap), BF16), own_out], axis=1
    )
    own_second = jnp.concatenate([own_out, own_router], axis=1)
    cut = experts * 2 // 5
    bounds = ((0, cut), (cut, experts))
    own_experts = [
        jnp.concatenate([expert_in[lo:hi], expert_out[lo:hi]], axis=2) for lo, hi in bounds
    ]
    first_weights = lax.all_gather(own_weights, "gx", axis=0)
    line_joined = after(direct_gather(own_joined, ny), *own_experts)
    own_second = after(own_second, line_joined)
    line_second = direct_gather(own_second, ny)
    ready = after(out_grad, line_second, bias, cosine, sine, normed_one)
    grad_steps = [gather_step((ready, ready), 0, ny)]
    rest_joined = lax.all_gather(line_joined, "gx", axis=0)
    rest_second = lax.all_gather(line_second, "gx", axis=0)
    wide = []
    for own in own_experts:
        wide.append(lax.all_gather(own, "gx", axis=1, tiled=True))


    out_column = (joined + LANES + gap) // width
    rest_block = lambda b: (0, jnp.maximum(b - 1, 0), 0, 0)
    joined_specs = [
        pl.BlockSpec((nx, depth, joined), lambda b: (0, 0, 0)),
        pl.BlockSpec((nx, pl.Squeezed(), depth, joined), rest_block),
    ]
    out_specs = [
        pl.BlockSpec((nx, depth, width), lambda b: (0, 0, out_column)),
        pl.BlockSpec((nx, pl.Squeezed(), depth, width), rest_block),
    ]
    held_joined = pltpu.VMEM((D, joined), BF16)
    held_out = pltpu.VMEM((D, width), BF16)
    query, kv = pl.pallas_call(
        project_kernel,
        grid=(ny,),
        in_specs=[
            whole((rows, D)),
            *joined_specs,
            whole((rows, LANES)),
            whole((rows, LANES)),
        ],
        out_specs=[
            pl.BlockSpec((rows, width), lambda b: (0, b)),
            pl.BlockSpec((rows, kv_width), lambda b: (0, b)),
        ],
        out_shape=[
            jax.ShapeDtypeStruct((rows, ny * width), BF16),
            jax.ShapeDtypeStruct((rows, ny * kv_width), BF16),
        ],
        scratch_shapes=[held_joined],
        compiler_params=params(),
        cost_estimate=cost(10),
        name="project",
    )(after(normed_one, bias), first_weights, rest_joined, cosine, sine)
    halo = lax.ppermute(kv[rows - SEGMAX :], "gy", [(s, s + 1) for s in range(ny - 1)])
    halves = rows // SEGMAX
    half_rows = lambda n, w: pl.BlockSpec((SEGMAX, w), lambda b: (n, b))
    whole_half = lambda n, w: pl.BlockSpec((SEGMAX, w), lambda b: (n, 0))
    below_rows = pl.BlockSpec((SEGMAX, kv_width), lambda b: (0, (b + ny - 1) % ny))
    bias_half = lambda n: pl.BlockSpec((pl.Squeezed(), 2 * SEGMAX, SEGMAX), lambda b: (n, 0, 0))

    def window(n):
        if n == 0:
            return [half_rows(0, kv_width), below_rows], (kv, halo)
        return [half_rows(n, kv_width), half_rows(n - 1, kv_width)], (kv, kv)

    mixed = [None] * halves
    for n in reversed(range(halves)):
        specs, arrays = window(n)
        mixed[n] = pl.pallas_call(
            attend_kernel,
            grid=(ny,),
            in_specs=[half_rows(n, width), *specs, bias_half(n)],
            out_specs=half_rows(0, width),
            out_shape=jax.ShapeDtypeStruct((SEGMAX, ny * width), BF16),
            compiler_params=params(),
            cost_estimate=cost(8),
            name="attend",
        )(query, *arrays, bias)
    for step in range(1, ny - 2):
        grad_steps.append(gather_step(grad_steps[-1], step, ny, mixed[-1]))
    middle, *normed_chunks = pl.pallas_call(
        functools.partial(branch_kernel, halves),
        grid=(1,),
        in_specs=[whole((SEGMAX, ny * width))] * halves
        + [
            out_specs[0],
            pl.BlockSpec((nx, ny - 1, depth, width), lambda _: (0, 0, 0, 0)),
            whole((rows, D)),
            whole((1, D)),
        ],
        out_specs=[whole((rows, D))] + [whole((CHUNK, D))] * own_chunks,
        out_shape=[jax.ShapeDtypeStruct((rows, D), F32)]
        + [jax.ShapeDtypeStruct((CHUNK, D), BF16)] * own_chunks,
        compiler_params=params(),
        cost_estimate=cost(7),
        name="branch",
    )(*mixed, first_weights, rest_second, tokens, moe_gain[None, :])

    router = jnp.concatenate(
        [
            first_weights[:, None, :, joined : joined + experts],
            rest_second[:, :, :, width : width + experts],
        ],
        axis=1,
    )
    router = router.transpose(0, 2, 1, 3).reshape(D, all_experts)
    router = jnp.pad(router, ((0, 0), (0, LANES - all_experts)))
    normed_two = jnp.concatenate(normed_chunks, axis=0)
    normed_steps = []
    for part in normed_chunks:
        part = after(part, grad_steps[-1])
        normed_steps.append([(part, part)])
    for step in range(ny - 1):
        for steps in normed_steps:
            steps.append(gather_step(steps[-1], step, ny))
    grad_steps.append(
        gather_step(grad_steps[-1], ny - 2, ny, *[steps[-1] for steps in normed_steps])
    )
    normed_pieces = []
    for part, steps in zip(normed_chunks, normed_steps):
        normed_pieces += [part] + [up for up, _ in steps[1:]] + [down for _, down in steps[1:]]
    grad_pieces = [out_grad] + [up for up, _ in grad_steps] + [down for _, down in grad_steps]
    smem = pl.BlockSpec(memory_space=pltpu.SMEM)
    vmem = pl.BlockSpec(memory_space=pltpu.VMEM)
    slot_rows = jax.ShapeDtypeStruct((experts, SLOTS, D), BF16)
    slot_lanes = lambda kind: jax.ShapeDtypeStruct((experts, SLOTS, LANES), kind)
    dispatch_scratch = lambda parts: [
        pltpu.VMEM((experts * SHORT_WINDOW, CHUNK), BF16),
        pltpu.VMEM((ny, rows, D), BF16),
        pltpu.SemaphoreType.DMA((ny, parts)),
    ]
    hbm = pl.BlockSpec(memory_space=pl.ANY)
    slot_grads = pl.pallas_call(
        functools.partial(dispatch_kernel, False, experts, ny),
        in_specs=[smem, smem] + [hbm] * (2 * ny - 1) + [vmem],
        out_specs=vmem,
        out_shape=slot_rows,
        scratch_shapes=dispatch_scratch(1),
        compiler_params=params(),
        cost_estimate=cost(26),
        name="dispatch_grads",
    )(pieces, ends, *grad_pieces, pos)
    dispatched, slot_gates = pl.pallas_call(
        functools.partial(dispatch_kernel, True, experts, ny),
        in_specs=[smem, smem] + [hbm] * len(normed_pieces) + [vmem] * 3,
        out_specs=[vmem, vmem],
        out_shape=[slot_rows, slot_lanes(F32)],
        scratch_shapes=dispatch_scratch(own_chunks),
        compiler_params=params(),
        cost_estimate=cost(31),
        name="dispatch_rows",
    )(pieces, ends, *normed_pieces, pos, router, members)

    half = (lax.axis_index("gx") % 2).reshape(1)
    y_rows, z_rows, slot_pairs, weight_terms = [], [], [], []
    for n, (lo, hi) in enumerate(bounds):
        outer = lambda *shape: pl.BlockSpec((1,) + shape, lambda e, lo=lo: (lo + e, 0, 0))
        inner = lambda *shape: pl.BlockSpec((1,) + shape, lambda e: (e, 0, 0))
        parts = n + 1
        slices = pl.BlockSpec((nx // parts, pl.Squeezed(), depth, 3 * FF), lambda e: (0, e, 0, 0))
        y, z, pair, *terms = pl.pallas_call(
            functools.partial(expert_kernel, lo, experts),
            grid=(hi - lo,),
            in_specs=[
                smem,
                outer(SLOTS, D),
                outer(SLOTS, D),
                outer(SLOTS, LANES),
                inner(D, 3 * FF),
            ],
            out_specs=[inner(SLOTS, D), inner(SLOTS, D), inner(SLOTS, LANES)]
            + [slices] * parts,
            out_shape=[
                jax.ShapeDtypeStruct((hi - lo, SLOTS, D), BF16),
                jax.ShapeDtypeStruct((hi - lo, SLOTS, D), BF16),
                jax.ShapeDtypeStruct((hi - lo, SLOTS, LANES), BF16),
            ]
            + [jax.ShapeDtypeStruct((nx // parts, hi - lo, depth, 3 * FF), BF16)] * parts,
            compiler_params=params(),
            cost_estimate=cost(9 * (hi - lo)),
            name="experts",
        )(half, dispatched, slot_grads, slot_gates, wide[n])
        y_rows.append(y)
        z_rows.append(z)
        slot_pairs.append(pair)
        weight_terms.append(terms)
    def combine(rows_in, which, pairs=None):
        held = pltpu.VMEM((3, experts * WINDOW, D), BF16)
        sems = pltpu.SemaphoreType.DMA((3, experts))
        hot_t = pltpu.VMEM((CHUNK, experts * WINDOW), BF16)
        total = pltpu.VMEM((CHUNK, D), F32)
        more = pairs is not None
        columns = D + LANES * more
        halves = chunks // ny
        here = pieces[jnp.array(which)]

        def place_map(c, piece_ref):
            return (piece_ref[c // halves] * halves + c % halves, 0)

        visits = 1 if more else halves

        def out_map(n):
            return lambda c, piece_ref: (jnp.clip(c - n * visits, 0, visits - 1), 0)

        return pl.pallas_call(
            functools.partial(combine_kernel, more, tuple(hi - lo for lo, hi in bounds), which),
            grid_spec=pltpu.PrefetchScalarGridSpec(
                num_scalar_prefetch=1,
                grid=(halves * len(which),),
                in_specs=[smem, pl.BlockSpec((CHUNK, LANES), place_map)]
                + [hbm] * len(bounds)
                + [once((hi - lo, SLOTS, LANES)) for lo, hi in bounds] * more,
                out_specs=[
                    pl.BlockSpec((CHUNK, columns), out_map(n))
                    for n in range(len(which) * halves // visits)
                ],
                scratch_shapes=[held, sems, hot_t, total]
                + [
                    pltpu.VMEM((experts * WINDOW, LANES), BF16),
                    pltpu.VMEM((CHUNK, LANES), F32),
                ]
                * more,
            ),
            out_shape=[jax.ShapeDtypeStruct((CHUNK * visits, columns), BF16)]
            * (len(which) * halves // visits),
            compiler_params=params(),
            cost_estimate=cost(16),
            name="combine_grads" if more else "combine_rows",
        )(here, ends, places, *rows_in, *(pairs if more else []))

    outer_pieces = sorted({1, ny - 1})
    inner_pieces = [k for k in range(ny) if k not in outer_pieces]
    order = outer_pieces + inner_pieces
    token_sum = combine(z_rows, order, slot_pairs)
    token_sum = [
        [token_sum[order.index(k) * own_chunks + n] for k in range(ny)] for n in range(own_chunks)
    ]
    token_steps = [[] for _ in token_sum]
    for step in range(1, ny):
        for parts, steps in zip(token_sum, token_steps):
            steps.append(sum_step(parts, steps[-1] if steps else None, step, ny))
    own_logits = jnp.where(own_members > 0.5, dot_nn(normed_two, router), MASKED)
    own_raised = jnp.exp(own_logits)
    own_gates = own_raised / jnp.sum(own_raised, axis=1, keepdims=True)
    source = lane_expert // (2 * experts) * experts + lane_expert % experts
    source = jnp.where(lane_expert < 2 * all_experts, source, -1)
    select = (source[:, None] == lane_expert[None, :]).astype(BF16)
    weight_sums = [
        lax.psum_scatter(weight_terms[0][0], "gx", scatter_dimension=0, tiled=True)[0],
        pair_scatter(*weight_terms[1], nx, token_sum[0][0]),
    ]
    combined = combine([after(y, [steps[-2] for steps in token_steps]) for y in y_rows], order)
    combined = [combined[order.index(k)] for k in range(ny)]
    row_block = lambda w: pl.BlockSpec((LANES, w), lambda r: (r, 0))
    later_block = lambda n, w: pl.BlockSpec((LANES, w), lambda r: (r + n * CHUNK // LANES, 0))
    backs = []
    for n, (parts, steps) in enumerate(zip(token_sum, token_steps)):
        backs.append(
            pl.pallas_call(
                middle_back_kernel,
                grid=(CHUNK // LANES,),
                in_specs=[row_block(D + LANES)] * 3
                + [later_block(n, LANES), whole((LANES, LANES)), whole((D, LANES))]
                + [later_block(n, D), whole((1, D)), later_block(n, D)],
                out_specs=[row_block(D), row_block(D), row_block(LANES), row_block(LANES)]
                + [whole((1, D))],
                out_shape=[
                    jax.ShapeDtypeStruct((CHUNK, D), F32),
                    jax.ShapeDtypeStruct((CHUNK, D), BF16),
                    jax.ShapeDtypeStruct((CHUNK, LANES), BF16),
                    jax.ShapeDtypeStruct((CHUNK, LANES), BF16),
                    jax.ShapeDtypeStruct((1, D), F32),
                ],
                compiler_params=params(),
                cost_estimate=cost(4),
                name="middle_back",
            )(after(parts[0], *combined), *steps[-1], own_gates, select, router, middle,
              moe_gain[None, :], out_grad)
        )
    middle_grads, branch_grads, highs, lows, moe_gain_grads = zip(*backs)
    moe_gain_grad = sum(moe_gain_grads)

    combined_steps = [sum_step(combined, None, 1, ny)]

    dquery, dkv, dbefore = [], [], []
    for n in range(halves):
        specs, arrays = window(n)
        outs = pl.pallas_call(
            attend_back_kernel,
            grid=(ny,),
            in_specs=[
                half_rows(n, width),
                *specs,
                bias_half(n),
                *out_specs,
                whole((SEGMAX, D)),
                whole_half(n, LANES),
                whole_half(n, LANES),
            ],
            out_specs=[half_rows(0, width), half_rows(0, kv_width), half_rows(0, kv_width)],
            out_shape=[
                jax.ShapeDtypeStruct((SEGMAX, ny * width), BF16),
                jax.ShapeDtypeStruct((SEGMAX, ny * kv_width), F32),
                jax.ShapeDtypeStruct((SEGMAX, ny * kv_width), F32 if n else BF16),
            ],
            scratch_shapes=[pltpu.VMEM((SEGMAX, width), F32), held_out],
            compiler_params=params(),
            cost_estimate=cost(17),
            name="attend_back",
        )(query, *arrays, bias, first_weights, rest_second, after(branch_grads[n], *combined, *dbefore),
          cosine, sine)
        for kept, out in zip((dquery, dkv, dbefore), outs):
            kept.append(out)
    halo_grad = lax.ppermute(dbefore[0], "gy", [(s + 1, s) for s in range(ny - 1)])
    second_term = pl.pallas_call(
        functools.partial(branch_weights_kernel, experts, halves),
        grid=(ny,),
        in_specs=[whole((D, rows))]
        + [whole((CHUNK, D))] * halves
        + [whole((CHUNK, LANES))] * (2 * halves)
        + [half_rows(0, width)] * halves,
        out_specs=pl.BlockSpec((nx, pl.Squeezed(), depth, width + LANES), lambda b: (0, b, 0, 0)),
        out_shape=jax.ShapeDtypeStruct((nx, ny, depth, width + LANES), BF16),
        scratch_shapes=[pltpu.VMEM((D, rows), BF16), pltpu.VMEM((D, LANES), F32)],
        compiler_params=params(),
        cost_estimate=cost(9),
        name="branch_weights",
    )(normed_two.T, *branch_grads, *highs, *lows, *mixed)
    added = ()
    for step in range(2, ny):
        gates = (halo_grad,) if step == 2 else ()
        added = sum_added(combined, combined_steps[-1], step, ny, *gates)
        combined_steps.append(sum_sent(added, step, ny))
    next_rows = pl.BlockSpec((SEGMAX, kv_width), lambda b: (0, (b + 1) % ny))
    *joined_terms, normed_one_grad = pl.pallas_call(
        functools.partial(project_back_kernel, halves),
        grid=(ny,),
        in_specs=[half_rows(0, width)] * halves
        + [half_rows(0, kv_width)] * (2 * halves - 1)
        + [
            next_rows,
            smem,
            whole((D, rows)),
            *joined_specs,
            whole((rows, LANES)),
            whole((rows, LANES)),
        ],
        out_specs=[pl.BlockSpec((nx // 2, pl.Squeezed(), depth, joined), lambda b: (0, b, 0, 0))] * 2
        + [whole((rows, D))],
        out_shape=[jax.ShapeDtypeStruct((nx // 2, ny, depth, joined), BF16)] * 2
        + [jax.ShapeDtypeStruct((rows, D), F32)],
        scratch_shapes=[held_joined],
        compiler_params=params(),
        cost_estimate=cost(22),
        name="project_back",
    )(*dquery, *dkv, *dbefore[1:], halo_grad, half, normed_one_t, first_weights, rest_joined, cosine,
      sine)
    in_grad, down_grad = [], []
    for part in after(tuple(weight_sums), joined_terms):
        in_grad.append(part[..., : 2 * FF].astype(F32))
        down_grad.append(part[..., 2 * FF :].astype(F32))
    in_grad, down_grad = jnp.concatenate(in_grad), jnp.concatenate(down_grad)
    last = tuple(after(part, in_grad, down_grad) for part in combined_steps[-1])
    layer_out = (middle + summed(combined, [last])).astype(BF16)
    input_grad, attn_gain_grad = pl.pallas_call(
        input_back_kernel,
        grid=(rows // LANES,),
        in_specs=[row_block(D), row_block(D), whole((1, D)), row_block(D)],
        out_specs=[row_block(D), whole((1, D))],
        out_shape=[
            jax.ShapeDtypeStruct((rows, D), F32),
            jax.ShapeDtypeStruct((1, D), F32),
        ],
        compiler_params=params(),
        cost_estimate=cost(6),
        name="input_back",
    )(tokens, normed_one_grad, attn_gain[None, :], after(jnp.concatenate(middle_grads), layer_out))

    second_sum = lax.psum_scatter(
        after(second_term, weight_sums[0]), "gx", scatter_dimension=0, tiled=True
    )
    second_sum = lax.optimization_barrier(second_sum)[0]
    mine, other = joined_terms
    other = after(other, combined_steps[1])
    joined_sum = pair_scatter(mine, other, nx, second_sum, *added, *weight_sums)
    gain_sums = jnp.concatenate([attn_gain_grad, moe_gain_grad])
    bit = 1
    while bit < nx:
        pairs = [(s, s ^ bit) for s in range(nx)]
        gain_sums = gain_sums + lax.ppermute(gain_sums, "gx", pairs)
        bit = 2 * bit
    high = gain_sums.astype(BF16)
    low = (gain_sums - high.astype(F32)).astype(BF16)
    gains = jnp.stack([high, low]).reshape(-1)
    gain_rows = -(-gains.shape[0] // joined)
    gain_rows += -gain_rows % SUBLANES
    gains = jnp.pad(gains, (0, gain_rows * joined - gains.shape[0])).reshape(gain_rows, joined)
    joined_sum = after(joined_sum, gains)
    joined_parts, gain_parts = [joined_sum[0]], [gains]
    for k in range(1, ny):
        part = jnp.concatenate([joined_sum[k], gains], axis=0)
        part = lax.ppermute(part, "gy", [(s, (s - k) % ny) for s in range(ny)])
        joined_parts.append(part)
        gain_parts.append(part[depth:])
    second_sum = direct_sum(second_sum, ny, *joined_parts[1:])
    out_weight_grad = second_sum[:, :heads_width].T
    router_grad = second_sum[:, width : width + experts].T
    qkv_grad = pl.pallas_call(
        functools.partial(joined_sum_kernel, groups),
        out_shape=jax.ShapeDtypeStruct(query_key_value_weight.shape, F32),
        compiler_params=params(),
        cost_estimate=cost(2),
        name="joined_sum",
    )(*joined_parts)
    gain_sums = jnp.roll(jnp.stack(gain_parts), me, axis=0).astype(F32)
    gain_sums = gain_sums.reshape(ny, -1)[:, : 4 * D].reshape(ny, 2, 2, D)
    gain_sums = jnp.sum(gain_sums, axis=(0, 1))
    return (
        layer_out,
        input_grad,
        gain_sums[0],
        qkv_grad,
        out_weight_grad,
        gain_sums[1],
        router_grad,
        in_grad,
        down_grad,
    )


def solution(mesh):
    in_specs = (
        P(("gx", "gy"), None),
        P(),
        P("gx", "gy"),
        P("gy", "gx"),
        P(),
        P("gy", "gx"),
        P("gy", "gx", None),
        P("gy", "gx", None),
        P("gx", None),
        P("gx", None),
        P("gx", None),
        P(("gx", "gy"), None),
    )
    out_specs = (
        P(("gx", "gy"), None),
        P(("gx", "gy"), None),
        P(),
        P("gx", "gy"),
        P("gy", "gx"),
        P(),
        P("gy", "gx"),
        P("gy", "gx", None),
        P("gy", "gx", None),
    )
    body = functools.partial(shards, mesh.shape["gx"], mesh.shape["gy"])
    return jax.shard_map(body, mesh=mesh, in_specs=in_specs, out_specs=out_specs, check_vma=False)
```

profile of v0, /device:TPU:0, one launch (start us, length us, event | category | flops | bytes accessed | tf_op | source)
XLA Modules:
  0.0 826.9 jit_solution(12398624421098837471)
XLA Ops:
  26.8 13.2 %collective-permute-done.1 = bf16[192,640]{0,1:T(8,128)(2,1)} collective-permute-done((bf16[192,640]{0,1:T(8,128)(2,1)}, bf16[192,640]{0,1:T(8,128)(2,1)}, u32[]{:S(2)}, u32[]{:S(2)}) %collective-permute-start.1) | collective-permute-done | bytes 245792 | tf_op jit(solution)/shard_map/ppermute | solution.py:622
  80.4 10.0 %collective-permute-start.7 = (bf16[512,1536]{1,0:T(8,128)(2,1)S(1)}, bf16[512,1536]{1,0:T(8,128)(2,1)}, u32[]{:S(2)}, u32[]{:S(2)}) collective-permute-start(bf16[512,1536]{1,0:T(8,128)(2,1)S(1)} %copy-done.43), channel_id=1, source_target_pairs={{0,1},{1,2},{2,3},{4,5},{5,6},{6,7},{8,9},{9,10},{10,11},{12,13},{... | collective-permute-start | bytes 4718600 | tf_op jit(solution)/shard_map/ppermute | solution.py:631
  95.1 11.2 %project.1 = (bf16[512,1536]{1,0:T(8,128)(2,1)}, bf16[512,1024]{1,0:T(8,128)(2,1)}) custom-call(bf16[512,1536]{1,0:T(8,128)(2,1)} %copy.95.normed_ref, bf16[8,192,1152]{2,1,0:T(8,128)(2,1)} %bitcast.113, bf16[8,3,192,640]{3,2,1,0:T(8,128)(2,1)} %bitcast.121, f32[512,128]{1,0:T(8,128)} %get-tuple-element.249.cos_ref.refs_10_, ...), custom_call_target="tpu_custom_call" | custom-call | flops 11000000512 | bytes 36000000 | tf_op jit(solution)/shard_map/project/pallas_call | solution.py:818
  143.5 9.7 %branch.1 = (f32[512,1536]{1,0:T(8,128)}, bf16[256,1536]{1,0:T(8,128)(2,1)}, bf16[256,1536]{1,0:T(8,128)(2,1)}) custom-call(bf16[256,1536]{1,0:T(8,128)(2,1)} %attend.2.refs_0_.refs_6_, bf16[256,1536]{1,0:T(8,128)(2,1)} %attend.3.refs_1_.refs_7_, bf16[8,192,1152]{2,1,0:T(8,128)(2,1)} %bitcast.114, bf16[8,3,192,512]{3,2,1,0:T(8,128)(2,1)} %bitcast.102, ...), custom_call_target="tpu_custom_call" | custom-call | flops 7699999744 | bytes 25200000 | tf_op jit(solution)/shard_map/branch/pallas_call | solution.py:867
  159.3 12.3 %collective-permute-start.17 = (bf16[256,1536]{1,0:T(8,128)(2,1)}, bf16[256,1536]{1,0:T(8,128)(2,1)S(1)}, u32[]{:S(2)}, u32[]{:S(2)}) collective-permute-start(bf16[256,1536]{1,0:T(8,128)(2,1)} %get-tuple-element.105.refs_9_), channel_id=1, source_target_pairs={{0,1},{1,2},{2,3},{4,5},{5,6},{6,7},{8,9},{9,10},{10,11},{12,13},{... | collective-permute-start | bytes 2359304 | tf_op jit(solution)/shard_map/ppermute | solution.py:631
  180.1 9.8 %collective-permute-done.17.refs_10_ = bf16[256,1536]{1,0:T(8,128)(2,1)S(1)} collective-permute-done((bf16[256,1536]{1,0:T(8,128)(2,1)}, bf16[256,1536]{1,0:T(8,128)(2,1)S(1)}, u32[]{:S(2)}, u32[]{:S(2)}) %collective-permute-start.17) | collective-permute-done | bytes 786464 | tf_op jit(solution)/shard_map/ppermute | solution.py:631
  214.8 13.6 %collective-permute-done.21.refs_14_ = bf16[256,1536]{1,0:T(8,128)(2,1)} collective-permute-done((bf16[256,1536]{1,0:T(8,128)(2,1)S(1)}, bf16[256,1536]{1,0:T(8,128)(2,1)}, u32[]{:S(2)}, u32[]{:S(2)}) %collective-permute-start.21) | collective-permute-done | bytes 786464 | tf_op jit(solution)/shard_map/ppermute | solution.py:632
  231.3 14.0 %collective-permute-done.15.refs_7_ = bf16[256,1536]{1,0:T(8,128)(2,1)} collective-permute-done((bf16[256,1536]{1,0:T(8,128)(2,1)}, bf16[256,1536]{1,0:T(8,128)(2,1)}, u32[]{:S(2)}, u32[]{:S(2)}) %collective-permute-start.15) | collective-permute-done | bytes 786464 | tf_op jit(solution)/shard_map/ppermute | solution.py:632
  246.6 11.5 %compare_reduce_fusion = pred[2048,128]{1,0:T(8,128)(4,1)S(1)} fusion(s32[128]{0:T(128)S(1)} %compare_select_fusion.5, s32[2048,8]{1,0:T(8,128)S(1)} %copy.102), kind=kLoop, calls=%fused_computation.2 | loop fusion | flops 3932160 | bytes 328192 | tf_op jit(solution)/shard_map/reduce_or | solution.py:744
  278.7 27.4 %dispatch_rows.1 = (bf16[10,464,1536]{2,1,0:T(8,128)(2,1)}, f32[10,464,128]{2,1,0:T(8,128)}) custom-call(s32[4]{0:T(128)} %and_select_fusion.6.refs_0_, s32[16,9]{1,0:T(8,128)} %bitcast.123, bf16[256,1536]{1,0:T(8,128)(2,1)} %get-tuple-element.103.refs_2_, bf16[256,1536]{1,0:T(8,128)(2,1)} %collective-permute-done.11.refs_3_, ...), custom_call_target="tpu_custom_call" | custom-call | flops 34100000768 | bytes 111600000 | tf_op jit(solution)/shard_map/dispatch_rows/pallas_call | solution.py:929
  315.1 19.7 %dispatch_grads.1.grad_ref = bf16[10,464,1536]{2,1,0:T(8,128)(2,1)} custom-call(s32[4]{0:T(128)} %and_select_fusion.6.refs_0_, s32[16,9]{1,0:T(8,128)} %bitcast.124, bf16[512,1536]{1,0:T(8,128)(2,1)} %grad_ref.3, bf16[512,1536]{1,0:T(8,128)(2,1)} %collective-permute-done.7.refs_3_, bf16[512,1536]{1,0:T(8,128)(2,1)} %collective-permute-done.8.refs_4_, ...), custom_call_target="tpu_custom_call" | custom-call | flops 28600000512 | bytes 93600000 | tf_op jit(solution)/shard_map/dispatch_grads/pallas_call | solution.py:919
  334.8 35.2 %experts.2 = (bf16[4,464,1536]{2,1,0:T(8,128)(2,1)}, bf16[4,464,1536]{2,1,0:T(8,128)(2,1)}, bf16[4,464,128]{2,1,0:T(8,128)(2,1)}, bf16[8,4,192,1536]{3,2,1,0:T(8,128)(2,1)}) custom-call(s32[1]{0:T(128)} %bitcast.20.half_ref.refs_6_, bf16[10,464,1536]{2,1,0:T(8,128)(2,1)} %get-tuple-element.106.x_ref, bf16[10,464,1536]{2,1,0:T(8,128)(2,1)} %dispatch_grads.1.grad_ref, ...), custom_call_target="tpu_custom_call" | custom-call | flops 39600001024 | bytes 129600000 | tf_op jit(solution)/shard_map/experts/pallas_call | solution.py:947
  378.0 54.2 %experts.3 = (bf16[6,464,1536]{2,1,0:T(8,128)(2,1)}, bf16[6,464,1536]{2,1,0:T(8,128)(2,1)}, bf16[6,464,128]{2,1,0:T(8,128)(2,1)}, bf16[4,6,192,1536]{3,2,1,0:T(8,128)(2,1)}, bf16[4,6,192,1536]{3,2,1,0:T(8,128)(2,1)}) custom-call(s32[1]{0:T(128)} %bitcast.20.half_ref.refs_6_, bf16[10,464,1536]{2,1,0:T(8,128)(2,1)} %get-tuple-element.106.x_ref, ...), custom_call_target="tpu_custom_call" | custom-call | flops 59399999488 | bytes 194400000 | tf_op jit(solution)/shard_map/experts/pallas_call | solution.py:947
  435.2 24.0 %combine_grads.1 = (bf16[256,1664]{1,0:T(8,128)(2,1)}, bf16[256,1664]{1,0:T(8,128)(2,1)}, bf16[256,1664]{1,0:T(8,128)(2,1)}, bf16[256,1664]{1,0:T(8,128)(2,1)}, ...) custom-call(s32[4]{0:T(128)} %gather_fusion, ...), custom_call_target="tpu_custom_call" | custom-call | flops 17600000000 | bytes 57600000 | tf_op jit(solution)/shard_map/combine_grads/pallas_call | solution.py:991
  459.2 16.5 %add_convert_fusion = bf16[4,6,192,1536]{3,2,1,0:T(8,128)(2,1)} fusion(bf16[4,6,192,1536]{3,2,1,0:T(8,128)(2,1)} %collective-permute-done.39, bf16[4,6,192,1536]{3,2,1,0:T(8,128)(2,1)} %get-tuple-element.135), kind=kLoop, calls=%fused_computation.1 | loop fusion | flops 28311552 | bytes 42467328 | tf_op jit(solution)/shard_map/convert_element_type | solution.py:613
  527.0 11.2 %collective-permute-done.30 = bf16[256,1664]{1,0:T(8,128)(2,1)S(1)} collective-permute-done((bf16[256,1664]{1,0:T(8,128)(2,1)S(1)}, bf16[256,1664]{1,0:T(8,128)(2,1)S(1)}, u32[]{:S(2)}, u32[]{:S(2)}) %collective-permute-start.30) | collective-permute-done | bytes 852000 | tf_op jit(solution)/shard_map/ppermute | solution.py:651
  544.6 11.8 %collective-permute-done.26 = bf16[256,1664]{1,0:T(8,128)(2,1)S(1)} collective-permute-done((bf16[256,1664]{1,0:T(8,128)(2,1)S(1)}, bf16[256,1664]{1,0:T(8,128)(2,1)S(1)}, u32[]{:S(2)}, u32[]{:S(2)}) %collective-permute-start.26) | collective-permute-done | bytes 852000 | tf_op jit(solution)/shard_map/ppermute | solution.py:651
  565.1 20.7 %combine_rows.1 = (bf16[512,1536]{1,0:T(8,128)(2,1)}, bf16[512,1536]{1,0:T(8,128)(2,1)}, bf16[512,1536]{1,0:T(8,128)(2,1)}, bf16[512,1536]{1,0:T(8,128)(2,1)}) custom-call(s32[4]{0:T(128)} %gather_fusion, s32[16,9]{1,0:T(8,128)} %bitcast.126, s32[2048,128]{1,0:T(8,128)} %pad.18.refs_2_, bf16[4,464,1536]{2,1,0:T(8,128)(2,1)} %get-tuple-element.121.refs_3_, ...), custom_call_target="tpu_custom_call" | custom-call | flops 17600000000 | bytes 57600000 | tf_op jit(solution)/shard_map/combine_rows/pallas_call | solution.py:991
  612.2 18.7 %attend_back.2 = (bf16[256,1536]{1,0:T(8,128)(2,1)}, f32[256,1024]{1,0:T(8,128)}, bf16[256,1024]{1,0:T(8,128)(2,1)}) custom-call(bf16[512,1536]{1,0:T(8,128)(2,1)} %get-tuple-element.93.query_ref, bf16[512,1024]{1,0:T(8,128)(2,1)} %get-tuple-element.94.own_ref.before_ref, bf16[256,1024]{1,0:T(8,128)(2,1)} %collective-permute-done.3.before_ref, ...), custom_call_target="tpu_custom_call" | custom-call | flops 18699999232 | bytes 61200000 | tf_op jit(solution)/shard_map/attend_back/pallas_call | solution.py:1074
  632.3 18.7 %attend_back.3 = (bf16[256,1536]{1,0:T(8,128)(2,1)}, f32[256,1024]{1,0:T(8,128)}, f32[256,1024]{1,0:T(8,128)}) custom-call(bf16[512,1536]{1,0:T(8,128)(2,1)} %get-tuple-element.93.query_ref, bf16[512,1024]{1,0:T(8,128)(2,1)} %get-tuple-element.94.own_ref.before_ref, bf16[512,1024]{1,0:T(8,128)(2,1)} %get-tuple-element.94.own_ref.before_ref, ...), custom_call_target="tpu_custom_call" | custom-call | flops 18699999232 | bytes 61200000 | tf_op jit(solution)/shard_map/attend_back/pallas_call | solution.py:1074
  662.4 24.5 %project_back.1 = (bf16[4,4,192,640]{3,2,1,0:T(8,128)(2,1)}, bf16[4,4,192,640]{3,2,1,0:T(8,128)(2,1)}, f32[512,1536]{1,0:T(8,128)}) custom-call(bf16[256,1536]{1,0:T(8,128)(2,1)} %get-tuple-element.138.refs_0_, bf16[256,1536]{1,0:T(8,128)(2,1)} %get-tuple-element.143.refs_1_, f32[256,1024]{1,0:T(8,128)} %get-tuple-element.144.refs_2_, ...), custom_call_target="tpu_custom_call" | custom-call | flops 24199999488 | bytes 79200000 | tf_op jit(solution)/shard_map/project_back/pallas_call | solution.py:1121
  707.4 11.4 %collective-permute-start.38 = (bf16[512,1536]{1,0:T(8,128)(2,1)}, bf16[512,1536]{1,0:T(8,128)(2,1)S(1)}, u32[]{:S(2)}, u32[]{:S(2)}) collective-permute-start(bf16[512,1536]{1,0:T(8,128)(2,1)} %add_convert_fusion.4), channel_id=1, source_target_pairs={{0,1},{1,2},{2,3},{4,5},{5,6},{6,7},{8,9},{9,10},{10,11},{12,13},{... | collective-permute-start | bytes 4718600 | tf_op jit(solution)/shard_map/ppermute | solution.py:651
  732.6 20.3 %collective-permute-done.38 = bf16[512,1536]{1,0:T(8,128)(2,1)S(1)} collective-permute-done((bf16[512,1536]{1,0:T(8,128)(2,1)}, bf16[512,1536]{1,0:T(8,128)(2,1)S(1)}, u32[]{:S(2)}, u32[]{:S(2)}) %collective-permute-start.38) | collective-permute-done | bytes 1572896 | tf_op jit(solution)/shard_map/ppermute | solution.py:651
  785.9 26.5 %collective-permute-done.50.refs_2_ = bf16[208,640]{1,0:T(8,128)(2,1)S(1)} collective-permute-done((bf16[208,640]{1,0:T(8,128)(2,1)S(1)}, bf16[208,640]{1,0:T(8,128)(2,1)S(1)}, u32[]{:S(2)}, u32[]{:S(2)}) %collective-permute-start.50) | collective-permute-done | bytes 266272 | tf_op jit(solution)/shard_map/ppermute | solution.py:1188
  (359 shorter events, 365.2 us)
Async XLA Ops:
  7.2 83.2 %all-gather.13.cloned.1.call-start = ((), (), s32[]{:S(2)}) async-start(), calls=%async_computation.8 | async-start | bytes 3981312 | tf_op jit(solution)/shard_map/all_gather | solution.py:793
  11.9 83.2 %all-gather.15.cloned.1.call-start = ((), (), s32[]{:S(2)}) async-start(), calls=%async_computation.9 | async-start | bytes 6635520 | tf_op jit(solution)/shard_map/all_gather | solution.py:799
  42.8 100.8 %all-gather.17.cloned.1.call-start = ((), (), s32[]{:S(2)}) async-start(), calls=%async_computation.10 | async-start | bytes 5308416 | tf_op jit(solution)/shard_map/all_gather | solution.py:800
  69.6 265.2 %all-gather.9.cloned.1.call-start = ((), (), s32[]{:S(2)}) async-start(), calls=%async_computation.4 | async-start | bytes 21233664 | tf_op jit(solution)/shard_map/all_gather | solution.py:803
  70.2 307.9 %all-gather.11.cloned.1.call-start = ((), (), s32[]{:S(2)}) async-start(), calls=%async_computation.5 | async-start | bytes 31850496 | tf_op jit(solution)/shard_map/all_gather | solution.py:803
  70.8 541.1 %reduce-scatter.9.cloned.1.call-start = ((), (), s32[]{:S(2)}) async-start(), calls=%async_computation.6 | async-start | bytes 21233664 | tf_op jit(solution)/shard_map/reduce_scatter | solution.py:1035
  79.1 42.6 %collective-permute-start.9 = (bf16[512,1536]{1,0:T(8,128)(2,1)S(1)}, bf16[512,1536]{1,0:T(8,128)(2,1)S(1)}, u32[]{:S(2)}, u32[]{:S(2)}) collective-permute-start(bf16[512,1536]{1,0:T(8,128)(2,1)S(1)} %copy-done.43), channel_id=1, source_target_pairs={{1,0},{2,1},{3,2},{5,4},{6,5},{7,6},{9,8},{10,9},{11,10},{13,12},{... | collective-permute-start | bytes 4718600 | tf_op jit(solution)/shard_map/ppermute | solution.py:632
  80.4 43.7 %collective-permute-start.7 = (bf16[512,1536]{1,0:T(8,128)(2,1)S(1)}, bf16[512,1536]{1,0:T(8,128)(2,1)}, u32[]{:S(2)}, u32[]{:S(2)}) collective-permute-start(bf16[512,1536]{1,0:T(8,128)(2,1)S(1)} %copy-done.43), channel_id=1, source_target_pairs={{0,1},{1,2},{2,3},{4,5},{5,6},{6,7},{8,9},{9,10},{10,11},{12,13},{... | collective-permute-start | bytes 4718600 | tf_op jit(solution)/shard_map/ppermute | solution.py:631
  121.7 37.6 %collective-permute-start.10 = (bf16[512,1536]{1,0:T(8,128)(2,1)S(1)}, bf16[512,1536]{1,0:T(8,128)(2,1)}, u32[]{:S(2)}, u32[]{:S(2)}) collective-permute-start(bf16[512,1536]{1,0:T(8,128)(2,1)S(1)} %collective-permute-done.9.refs_6_), channel_id=1, source_target_pairs={{1,0},{2,1},{5,4},{6,5},{9,8},{10,9},{13,12},{14,13},{17,16},{18,1... | collective-permute-start | bytes 4718600 | tf_op jit(solution)/shard_map/ppermute | solution.py:632
  213.3 57.1 %collective-permute-start.19 = (bf16[256,1536]{1,0:T(8,128)(2,1)}, bf16[256,1536]{1,0:T(8,128)(2,1)}, u32[]{:S(2)}, u32[]{:S(2)}) collective-permute-start(bf16[256,1536]{1,0:T(8,128)(2,1)} %collective-permute-done.18.refs_11_), channel_id=1, source_target_pairs={{2,3},{6,7},{10,11},{14,15},{18,19},{22,23},{26,27},{30,31}} | collective-permute-start | bytes 2359304 | tf_op jit(solution)/shard_map/ppermute | solution.py:631
  228.4 41.9 %collective-permute-start.22 = (bf16[256,1536]{1,0:T(8,128)(2,1)}, bf16[256,1536]{1,0:T(8,128)(2,1)}, u32[]{:S(2)}, u32[]{:S(2)}) collective-permute-start(bf16[256,1536]{1,0:T(8,128)(2,1)} %collective-permute-done.21.refs_14_), channel_id=1, source_target_pairs={{1,0},{5,4},{9,8},{13,12},{17,16},{21,20},{25,24},{29,28}} | collective-permute-start | bytes 2359304 | tf_op jit(solution)/shard_map/ppermute | solution.py:632
  229.7 40.6 %collective-permute-start.13 = (bf16[256,1536]{1,0:T(8,128)(2,1)}, bf16[256,1536]{1,0:T(8,128)(2,1)}, u32[]{:S(2)}, u32[]{:S(2)}) collective-permute-start(bf16[256,1536]{1,0:T(8,128)(2,1)} %collective-permute-done.12.refs_4_), channel_id=1, source_target_pairs={{2,3},{6,7},{10,11},{14,15},{18,19},{22,23},{26,27},{30,31}} | collective-permute-start | bytes 2359304 | tf_op jit(solution)/shard_map/ppermute | solution.py:631
  276.6 36.1 %collective-permute-start.24 = (bf16[512,1536]{1,0:T(8,128)(2,1)}, bf16[512,1536]{1,0:T(8,128)(2,1)S(1)}, u32[]{:S(2)}, u32[]{:S(2)}) collective-permute-start(bf16[512,1536]{1,0:T(8,128)(2,1)} %collective-permute-done.10.refs_7_), channel_id=1, source_target_pairs={{1,0},{5,4},{9,8},{13,12},{17,16},{21,20},{25,24},{29,28}} | collective-permute-start | bytes 4718600 | tf_op jit(solution)/shard_map/ppermute | solution.py:632
  370.0 328.2 %reduce-scatter.13.cloned.1.call-start = ((), (), s32[]{:S(2)}) async-start(), calls=%async_computation.11 | async-start | bytes 17694720
  475.8 293.2 %reduce-scatter.11.cloned.1.call-start = ((), (), s32[]{:S(2)}) async-start(), calls=%async_computation.7 | async-start | bytes 7077888 | tf_op jit(solution)/shard_map/reduce_scatter | solution.py:1165
  520.3 36.2 %collective-permute-start.26 = (bf16[256,1664]{1,0:T(8,128)(2,1)S(1)}, bf16[256,1664]{1,0:T(8,128)(2,1)S(1)}, u32[]{:S(2)}, u32[]{:S(2)}) collective-permute-start(bf16[256,1664]{1,0:T(8,128)(2,1)S(1)} %get-tuple-element.229), channel_id=1, source_target_pairs={{0,1},{1,2},{4,5},{5,6},{8,9},{9,10},{12,13},{13,14},{16,17},{17,1... | collective-permute-start | bytes 2555912 | tf_op jit(solution)/shard_map/ppermute | solution.py:651
  525.7 72.0 %collective-permute-start.41 = (bf16[256,1664]{1,0:T(8,128)(2,1)S(1)}, bf16[256,1664]{1,0:T(8,128)(2,1)}, u32[]{:S(2)}, u32[]{:S(2)}) collective-permute-start(bf16[256,1664]{1,0:T(8,128)(2,1)S(1)} %add_convert_fusion.5), channel_id=1, source_target_pairs={{3,2},{2,1},{1,0},{7,6},{6,5},{5,4},{11,10},{10,9},{9,8},{15,14},{... | collective-permute-start | bytes 2555912 | tf_op jit(solution)/shard_map/ppermute | solution.py:652
  539.3 58.4 %collective-permute-start.40 = (bf16[256,1664]{1,0:T(8,128)(2,1)}, bf16[256,1664]{1,0:T(8,128)(2,1)}, u32[]{:S(2)}, u32[]{:S(2)}) collective-permute-start(bf16[256,1664]{1,0:T(8,128)(2,1)} %add_convert_fusion.6), channel_id=1, source_target_pairs={{0,1},{1,2},{2,3},{4,5},{5,6},{6,7},{8,9},{9,10},{10,11},{12,13},{... | collective-permute-start | bytes 2555912 | tf_op jit(solution)/shard_map/ppermute | solution.py:651
  585.8 65.1 %collective-permute-start.42 = (bf16[512,1536]{1,0:T(8,128)(2,1)}, bf16[512,1536]{1,0:T(8,128)(2,1)S(1)}, u32[]{:S(2)}, u32[]{:S(2)}) collective-permute-start(bf16[512,1536]{1,0:T(8,128)(2,1)} %get-tuple-element.125), channel_id=1, source_target_pairs={{3,2},{7,6},{11,10},{15,14},{19,18},{23,22},{27,26},{31,30}} | collective-permute-start | bytes 4718600 | tf_op jit(solution)/shard_map/ppermute | solution.py:652
  586.6 64.4 %collective-permute-start.33 = (bf16[512,1536]{1,0:T(8,128)(2,1)}, bf16[512,1536]{1,0:T(8,128)(2,1)}, u32[]{:S(2)}, u32[]{:S(2)}) collective-permute-start(bf16[512,1536]{1,0:T(8,128)(2,1)} %get-tuple-element.127), channel_id=1, source_target_pairs={{0,1},{4,5},{8,9},{12,13},{16,17},{20,21},{24,25},{28,29}} | collective-permute-start | bytes 4718600 | tf_op jit(solution)/shard_map/ppermute | solution.py:651
  611.9 164.2 %reduce-scatter.15.cloned.1.call-start = ((), (), s32[]{:S(2)}) async-start(), calls=%async_computation.12 | async-start | bytes 4915200
  655.0 38.7 %collective-permute-start.37 = (bf16[512,1536]{1,0:T(8,128)(2,1)}, bf16[512,1536]{1,0:T(8,128)(2,1)S(1)}, u32[]{:S(2)}, u32[]{:S(2)}) collective-permute-start(bf16[512,1536]{1,0:T(8,128)(2,1)} %get-tuple-element.220), channel_id=1, source_target_pairs={{0,1},{1,2},{4,5},{5,6},{8,9},{9,10},{12,13},{13,14},{16,17},{17,1... | collective-permute-start | bytes 4718600 | tf_op jit(solution)/shard_map/ppermute | solution.py:651
  707.4 45.6 %collective-permute-start.38 = (bf16[512,1536]{1,0:T(8,128)(2,1)}, bf16[512,1536]{1,0:T(8,128)(2,1)S(1)}, u32[]{:S(2)}, u32[]{:S(2)}) collective-permute-start(bf16[512,1536]{1,0:T(8,128)(2,1)} %add_convert_fusion.4), channel_id=1, source_target_pairs={{0,1},{1,2},{2,3},{4,5},{5,6},{6,7},{8,9},{9,10},{10,11},{12,13},{... | collective-permute-start | bytes 4718600 | tf_op jit(solution)/shard_map/ppermute | solution.py:651
  718.8 38.2 %collective-permute-start.44 = (bf16[512,1536]{1,0:T(8,128)(2,1)}, bf16[512,1536]{1,0:T(8,128)(2,1)S(1)}, u32[]{:S(2)}, u32[]{:S(2)}) collective-permute-start(bf16[512,1536]{1,0:T(8,128)(2,1)} %add_convert_fusion.3), channel_id=1, source_target_pairs={{3,2},{2,1},{1,0},{7,6},{6,5},{5,4},{11,10},{10,9},{9,8},{15,14},{... | collective-permute-start | bytes 4718600 | tf_op jit(solution)/shard_map/ppermute | solution.py:652
  (93 other events, 1829.3 us)
Sparse Core Ops, SparseCore 0:
  12.0 36.6 all-gather.12
  51.2 43.8 all-gather.14
  97.0 38.9 all-gather.16
  138.3 98.7 all-gather.8
  239.4 138.6 all-gather.10
  381.5 126.1 reduce-scatter.8
  510.8 133.6 reduce-scatter.12
  647.8 61.7 reduce-scatter.10
  713.0 50.6 reduce-scatter.14
where the time goes:
time: 837 us; the launch traced here: 827 us
  Pallas kernels  313 us (37%)
  waiting for transfers between devices  236 us (28%)
  starting transfers between devices  140 us (17%)
  other arithmetic  82.1 us (10%)
  local copies, waits for them, and re-layouts  40.1 us (5%)
  between operations  15.5 us (2%)
    pallas_call x2, Pallas kernels, shards(): pl.pallas_call(functools.partial(expert_kernel, lo, experts), grid=(hi -...  89.4 us
    ppermute x9, waiting for transfers between devices, sum_sent(): lax.ppermute(above, 'gy', [(s, s + 1) for s in range(step)])  66.8 us
    ppermute x9, waiting for transfers between devices, gather_step(): lax.ppermute(down, 'gy', [(s + 1, s) for s in range(0, size - 1 - step)])  56.2 us
    ppermute x9, starting transfers between devices, sum_sent(): lax.ppermute(above, 'gy', [(s, s + 1) for s in range(step)])  48.9 us
    pallas_call x2, Pallas kernels, combine(): pl.pallas_call(functools.partial(combine_kernel, more, tuple((hi - lo for...  44.7 us
    pallas_call x2, Pallas kernels, shards(): pl.pallas_call(attend_back_kernel, grid=(ny,), in_specs=[half_rows(n, wid...  37.3 us
    ppermute x9, starting transfers between devices, gather_step(): lax.ppermute(up, 'gy', [(s, s + 1) for s in range(step, size - 1)])  37.2 us
    ppermute x6, waiting for transfers between devices, direct_gather(): lax.ppermute(part, 'gy', [(s, (s + k) % size) for s in range(size)])  29.7 us
  transfers between devices with their start and end apart: 64, of which 33 were waited for; matrix products, arithmetic and copies ran while one was open for 13% of the time, Pallas kernels for 38%

commit v1 on v0

--- a/solution.py
+++ b/solution.py
@@ -1093,7 +1093,7 @@
             compiler_params=params(),
             cost_estimate=cost(17),
             name="attend_back",
-        )(query, *arrays, bias, first_weights, rest_second, after(branch_grads[n], *combined, *dbefore),
+        )(query, *arrays, bias, first_weights, rest_second, after(branch_grads[n], *branch_grads, *combined, *dbefore),
           cosine, sine)
         for kept, out in zip((dquery, dkv, dbefore), outs):
             kept.append(out)
@@ -1160,16 +1160,16 @@
         compiler_params=params(),
         cost_estimate=cost(6),
         name="input_back",
-    )(tokens, normed_one_grad, attn_gain[None, :], after(jnp.concatenate(middle_grads), layer_out))
+    )(tokens, normed_one_grad, attn_gain[None, :], jnp.concatenate(middle_grads))
 
     second_sum = lax.psum_scatter(
         after(second_term, weight_sums[0]), "gx", scatter_dimension=0, tiled=True
     )
     second_sum = lax.optimization_barrier(second_sum)[0]
     mine, other = joined_terms
-    other = after(other, combined_steps[1])
+    other = after(other, combined_steps[1], attn_gain_grad)
     joined_sum = pair_scatter(mine, other, nx, second_sum, *added, *weight_sums)
-    gain_sums = jnp.concatenate([attn_gain_grad, moe_gain_grad])
+    gain_sums = after(jnp.concatenate([attn_gain_grad, moe_gain_grad]), layer_out)
     bit = 1
     while bit < nx:
         pairs = [(s, s ^ bit) for s in range(nx)]

time: 837 us -> 827 us (0.988)
  transfers between devices with their start and end apart: 64 -> 64, of which waited for: 33 -> 32; matrix products, arithmetic and copies ran while one was open for 13% -> 13% of each run, Pallas kernels for 38% -> 38%
where the time goes in v1:
time: 827 us; the launch traced here: 817 us
  Pallas kernels  314 us (38%)
  waiting for transfers between devices  233 us (28%)
  starting transfers between devices  136 us (16%)
  other arithmetic  79.4 us (10%)
  local copies, waits for them, and re-layouts  38.7 us (5%)
  between operations  15.5 us (2%)
    pallas_call x2, Pallas kernels, shards(): pl.pallas_call(functools.partial(expert_kernel, lo, experts), grid=(hi -...  89.5 us
    ppermute x9, waiting for transfers between devices, sum_sent(): lax.ppermute(above, 'gy', [(s, s + 1) for s in range(step)])  62.9 us
    ppermute x9, waiting for transfers between devices, gather_step(): lax.ppermute(down, 'gy', [(s + 1, s) for s in range(0, size - 1 - step)])  56.4 us
    pallas_call x2, Pallas kernels, combine(): pl.pallas_call(functools.partial(combine_kernel, more, tuple((hi - lo for...  44.8 us
    ppermute x9, starting transfers between devices, sum_sent(): lax.ppermute(above, 'gy', [(s, s + 1) for s in range(step)])  42.4 us
    pallas_call x2, Pallas kernels, shards(): pl.pallas_call(attend_back_kernel, grid=(ny,), in_specs=[half_rows(n, wid...  38.6 us
    ppermute x9, starting transfers between devices, gather_step(): lax.ppermute(up, 'gy', [(s, s + 1) for s in range(step, size - 1)])  37.2 us
    ppermute x6, waiting for transfers between devices, direct_gather(): lax.ppermute(part, 'gy', [(s, (s + k) % size) for s in range(size)])  29.7 us
  transfers between devices with their start and end apart: 64, of which 32 were waited for; matrix products, arithmetic and copies ran while one was open for 13% of the time, Pallas kernels for 38%

profile of v1, /device:TPU:0, one launch (start us, length us, event | category | flops | bytes accessed | tf_op | source)
XLA Modules:
  0.0 817.2 jit_solution(1710823705160661902)
XLA Ops:
  26.8 13.2 %collective-permute-done.1 = bf16[192,640]{0,1:T(8,128)(2,1)} collective-permute-done((bf16[192,640]{0,1:T(8,128)(2,1)}, bf16[192,640]{0,1:T(8,128)(2,1)}, u32[]{:S(2)}, u32[]{:S(2)}) %collective-permute-start.1) | collective-permute-done | bytes 245792 | tf_op jit(solution)/shard_map/ppermute | solution.py:622
  58.9 9.4 %collective-permute-done.5 = bf16[192,512]{0,1:T(8,128)(2,1)S(1)} collective-permute-done((bf16[192,512]{0,1:T(8,128)(2,1)S(1)}, bf16[192,512]{0,1:T(8,128)(2,1)S(1)}, u32[]{:S(2)}, u32[]{:S(2)}) %collective-permute-start.5) | collective-permute-done | bytes 196640 | tf_op jit(solution)/shard_map/ppermute | solution.py:622
  80.3 10.0 %collective-permute-start.7 = (bf16[512,1536]{1,0:T(8,128)(2,1)S(1)}, bf16[512,1536]{1,0:T(8,128)(2,1)}, u32[]{:S(2)}, u32[]{:S(2)}) collective-permute-start(bf16[512,1536]{1,0:T(8,128)(2,1)S(1)} %copy-done.43), channel_id=1, source_target_pairs={{0,1},{1,2},{2,3},{4,5},{5,6},{6,7},{8,9},{9,10},{10,11},{12,13},{... | collective-permute-start | bytes 4718600 | tf_op jit(solution)/shard_map/ppermute | solution.py:631
  95.1 11.2 %project.1 = (bf16[512,1536]{1,0:T(8,128)(2,1)}, bf16[512,1024]{1,0:T(8,128)(2,1)}) custom-call(bf16[512,1536]{1,0:T(8,128)(2,1)} %copy.95.normed_ref, bf16[8,192,1152]{2,1,0:T(8,128)(2,1)} %bitcast.113, bf16[8,3,192,640]{3,2,1,0:T(8,128)(2,1)} %bitcast.121, f32[512,128]{1,0:T(8,128)} %get-tuple-element.249.cos_ref.refs_10_, ...), custom_call_target="tpu_custom_call" | custom-call | flops 11000000512 | bytes 36000000 | tf_op jit(solution)/shard_map/project/pallas_call | solution.py:818
  143.5 9.5 %branch.1 = (f32[512,1536]{1,0:T(8,128)}, bf16[256,1536]{1,0:T(8,128)(2,1)}, bf16[256,1536]{1,0:T(8,128)(2,1)}) custom-call(bf16[256,1536]{1,0:T(8,128)(2,1)} %attend.2.refs_0_.refs_6_, bf16[256,1536]{1,0:T(8,128)(2,1)} %attend.3.refs_1_.refs_7_, bf16[8,192,1152]{2,1,0:T(8,128)(2,1)} %bitcast.114, bf16[8,3,192,512]{3,2,1,0:T(8,128)(2,1)} %bitcast.102, ...), custom_call_target="tpu_custom_call" | custom-call | flops 7699999744 | bytes 25200000 | tf_op jit(solution)/shard_map/branch/pallas_call | solution.py:867
  159.3 12.3 %collective-permute-start.17 = (bf16[256,1536]{1,0:T(8,128)(2,1)}, bf16[256,1536]{1,0:T(8,128)(2,1)S(1)}, u32[]{:S(2)}, u32[]{:S(2)}) collective-permute-start(bf16[256,1536]{1,0:T(8,128)(2,1)} %get-tuple-element.105.refs_9_), channel_id=1, source_target_pairs={{0,1},{1,2},{2,3},{4,5},{5,6},{6,7},{8,9},{9,10},{10,11},{12,13},{... | collective-permute-start | bytes 2359304 | tf_op jit(solution)/shard_map/ppermute | solution.py:631
  180.1 9.8 %collective-permute-done.17.refs_10_ = bf16[256,1536]{1,0:T(8,128)(2,1)S(1)} collective-permute-done((bf16[256,1536]{1,0:T(8,128)(2,1)}, bf16[256,1536]{1,0:T(8,128)(2,1)S(1)}, u32[]{:S(2)}, u32[]{:S(2)}) %collective-permute-start.17) | collective-permute-done | bytes 786464 | tf_op jit(solution)/shard_map/ppermute | solution.py:631
  214.8 13.6 %collective-permute-done.21.refs_14_ = bf16[256,1536]{1,0:T(8,128)(2,1)} collective-permute-done((bf16[256,1536]{1,0:T(8,128)(2,1)S(1)}, bf16[256,1536]{1,0:T(8,128)(2,1)}, u32[]{:S(2)}, u32[]{:S(2)}) %collective-permute-start.21) | collective-permute-done | bytes 786464 | tf_op jit(solution)/shard_map/ppermute | solution.py:632
  231.3 14.0 %collective-permute-done.15.refs_7_ = bf16[256,1536]{1,0:T(8,128)(2,1)} collective-permute-done((bf16[256,1536]{1,0:T(8,128)(2,1)}, bf16[256,1536]{1,0:T(8,128)(2,1)}, u32[]{:S(2)}, u32[]{:S(2)}) %collective-permute-start.15) | collective-permute-done | bytes 786464 | tf_op jit(solution)/shard_map/ppermute | solution.py:632
  246.6 11.5 %compare_reduce_fusion = pred[2048,128]{1,0:T(8,128)(4,1)S(1)} fusion(s32[128]{0:T(128)S(1)} %compare_select_fusion.5, s32[2048,8]{1,0:T(8,128)S(1)} %copy.102), kind=kLoop, calls=%fused_computation.2 | loop fusion | flops 3932160 | bytes 328192 | tf_op jit(solution)/shard_map/reduce_or | solution.py:744
  278.7 27.4 %dispatch_rows.1 = (bf16[10,464,1536]{2,1,0:T(8,128)(2,1)}, f32[10,464,128]{2,1,0:T(8,128)}) custom-call(s32[4]{0:T(128)} %and_select_fusion.6.refs_0_, s32[16,9]{1,0:T(8,128)} %bitcast.123, bf16[256,1536]{1,0:T(8,128)(2,1)} %get-tuple-element.103.refs_2_, bf16[256,1536]{1,0:T(8,128)(2,1)} %collective-permute-done.11.refs_3_, ...), custom_call_target="tpu_custom_call" | custom-call | flops 34100000768 | bytes 111600000 | tf_op jit(solution)/shard_map/dispatch_rows/pallas_call | solution.py:929
  315.0 19.7 %dispatch_grads.1.grad_ref = bf16[10,464,1536]{2,1,0:T(8,128)(2,1)} custom-call(s32[4]{0:T(128)} %and_select_fusion.6.refs_0_, s32[16,9]{1,0:T(8,128)} %bitcast.124, bf16[512,1536]{1,0:T(8,128)(2,1)} %grad_ref.3, bf16[512,1536]{1,0:T(8,128)(2,1)} %collective-permute-done.7.refs_3_, bf16[512,1536]{1,0:T(8,128)(2,1)} %collective-permute-done.8.refs_4_, ...), custom_call_target="tpu_custom_call" | custom-call | flops 28600000512 | bytes 93600000 | tf_op jit(solution)/shard_map/dispatch_grads/pallas_call | solution.py:919
  334.8 35.2 %experts.2 = (bf16[4,464,1536]{2,1,0:T(8,128)(2,1)}, bf16[4,464,1536]{2,1,0:T(8,128)(2,1)}, bf16[4,464,128]{2,1,0:T(8,128)(2,1)}, bf16[8,4,192,1536]{3,2,1,0:T(8,128)(2,1)}) custom-call(s32[1]{0:T(128)} %bitcast.20.half_ref.refs_6_, bf16[10,464,1536]{2,1,0:T(8,128)(2,1)} %get-tuple-element.106.x_ref, bf16[10,464,1536]{2,1,0:T(8,128)(2,1)} %dispatch_grads.1.grad_ref, ...), custom_call_target="tpu_custom_call" | custom-call | flops 39600001024 | bytes 129600000 | tf_op jit(solution)/shard_map/experts/pallas_call | solution.py:947
  378.0 54.2 %experts.3 = (bf16[6,464,1536]{2,1,0:T(8,128)(2,1)}, bf16[6,464,1536]{2,1,0:T(8,128)(2,1)}, bf16[6,464,128]{2,1,0:T(8,128)(2,1)}, bf16[4,6,192,1536]{3,2,1,0:T(8,128)(2,1)}, bf16[4,6,192,1536]{3,2,1,0:T(8,128)(2,1)}) custom-call(s32[1]{0:T(128)} %bitcast.20.half_ref.refs_6_, bf16[10,464,1536]{2,1,0:T(8,128)(2,1)} %get-tuple-element.106.x_ref, ...), custom_call_target="tpu_custom_call" | custom-call | flops 59399999488 | bytes 194400000 | tf_op jit(solution)/shard_map/experts/pallas_call | solution.py:947
  435.1 24.0 %combine_grads.1 = (bf16[256,1664]{1,0:T(8,128)(2,1)}, bf16[256,1664]{1,0:T(8,128)(2,1)}, bf16[256,1664]{1,0:T(8,128)(2,1)}, bf16[256,1664]{1,0:T(8,128)(2,1)}, ...) custom-call(s32[4]{0:T(128)} %gather_fusion, ...), custom_call_target="tpu_custom_call" | custom-call | flops 17600000000 | bytes 57600000 | tf_op jit(solution)/shard_map/combine_grads/pallas_call | solution.py:991
  459.1 16.5 %add_convert_fusion = bf16[4,6,192,1536]{3,2,1,0:T(8,128)(2,1)} fusion(bf16[4,6,192,1536]{3,2,1,0:T(8,128)(2,1)} %collective-permute-done.41, bf16[4,6,192,1536]{3,2,1,0:T(8,128)(2,1)} %get-tuple-element.138), kind=kLoop, calls=%fused_computation.1 | loop fusion | flops 28311552 | bytes 42467328 | tf_op jit(solution)/shard_map/convert_element_type | solution.py:613
  526.9 11.2 %collective-permute-done.30 = bf16[256,1664]{1,0:T(8,128)(2,1)S(1)} collective-permute-done((bf16[256,1664]{1,0:T(8,128)(2,1)S(1)}, bf16[256,1664]{1,0:T(8,128)(2,1)S(1)}, u32[]{:S(2)}, u32[]{:S(2)}) %collective-permute-start.30) | collective-permute-done | bytes 852000 | tf_op jit(solution)/shard_map/ppermute | solution.py:651
  543.6 12.8 %collective-permute-done.26 = bf16[256,1664]{1,0:T(8,128)(2,1)S(1)} collective-permute-done((bf16[256,1664]{1,0:T(8,128)(2,1)S(1)}, bf16[256,1664]{1,0:T(8,128)(2,1)S(1)}, u32[]{:S(2)}, u32[]{:S(2)}) %collective-permute-start.26) | collective-permute-done | bytes 852000 | tf_op jit(solution)/shard_map/ppermute | solution.py:651
  564.0 20.8 %combine_rows.1 = (bf16[512,1536]{1,0:T(8,128)(2,1)}, bf16[512,1536]{1,0:T(8,128)(2,1)}, bf16[512,1536]{1,0:T(8,128)(2,1)}, bf16[512,1536]{1,0:T(8,128)(2,1)}) custom-call(s32[4]{0:T(128)} %gather_fusion, s32[16,9]{1,0:T(8,128)} %bitcast.126, s32[2048,128]{1,0:T(8,128)} %pad.18.refs_2_, bf16[4,464,1536]{2,1,0:T(8,128)(2,1)} %get-tuple-element.121.refs_3_, ...), custom_call_target="tpu_custom_call" | custom-call | flops 17600000000 | bytes 57600000 | tf_op jit(solution)/shard_map/combine_rows/pallas_call | solution.py:991
  601.3 19.8 %attend_back.2 = (bf16[256,1536]{1,0:T(8,128)(2,1)}, f32[256,1024]{1,0:T(8,128)}, bf16[256,1024]{1,0:T(8,128)(2,1)}) custom-call(bf16[512,1536]{1,0:T(8,128)(2,1)} %get-tuple-element.93.query_ref, bf16[512,1024]{1,0:T(8,128)(2,1)} %get-tuple-element.94.own_ref.before_ref, bf16[256,1024]{1,0:T(8,128)(2,1)} %collective-permute-done.3.before_ref, ...), custom_call_target="tpu_custom_call" | custom-call | flops 18699999232 | bytes 61200000 | tf_op jit(solution)/shard_map/attend_back/pallas_call | solution.py:1074
  631.6 18.8 %attend_back.3 = (bf16[256,1536]{1,0:T(8,128)(2,1)}, f32[256,1024]{1,0:T(8,128)}, f32[256,1024]{1,0:T(8,128)}) custom-call(bf16[512,1536]{1,0:T(8,128)(2,1)} %get-tuple-element.93.query_ref, bf16[512,1024]{1,0:T(8,128)(2,1)} %get-tuple-element.94.own_ref.before_ref, bf16[512,1024]{1,0:T(8,128)(2,1)} %get-tuple-element.94.own_ref.before_ref, ...), custom_call_target="tpu_custom_call" | custom-call | flops 18699999232 | bytes 61200000 | tf_op jit(solution)/shard_map/attend_back/pallas_call | solution.py:1074
  663.4 24.3 %project_back.1 = (bf16[4,4,192,640]{3,2,1,0:T(8,128)(2,1)}, bf16[4,4,192,640]{3,2,1,0:T(8,128)(2,1)}, f32[512,1536]{1,0:T(8,128)}) custom-call(bf16[256,1536]{1,0:T(8,128)(2,1)} %get-tuple-element.141.refs_0_, bf16[256,1536]{1,0:T(8,128)(2,1)} %get-tuple-element.143.refs_1_, f32[256,1024]{1,0:T(8,128)} %get-tuple-element.144.refs_2_, ...), custom_call_target="tpu_custom_call" | custom-call | flops 24199999488 | bytes 79200000 | tf_op jit(solution)/shard_map/project_back/pallas_call | solution.py:1121
  724.6 23.6 %collective-permute-done.40 = bf16[512,1536]{1,0:T(8,128)(2,1)S(1)} collective-permute-done((bf16[512,1536]{1,0:T(8,128)(2,1)}, bf16[512,1536]{1,0:T(8,128)(2,1)S(1)}, u32[]{:S(2)}, u32[]{:S(2)}) %collective-permute-start.40) | collective-permute-done | bytes 1572896 | tf_op jit(solution)/shard_map/ppermute | solution.py:651
  776.2 25.6 %collective-permute-done.50.refs_2_ = bf16[208,640]{1,0:T(8,128)(2,1)S(1)} collective-permute-done((bf16[208,640]{1,0:T(8,128)(2,1)S(1)}, bf16[208,640]{1,0:T(8,128)(2,1)S(1)}, u32[]{:S(2)}, u32[]{:S(2)}) %collective-permute-start.50) | collective-permute-done | bytes 266272 | tf_op jit(solution)/shard_map/ppermute | solution.py:1188
  (357 shorter events, 353.2 us)
Async XLA Ops:
  7.2 83.2 %all-gather.13.cloned.1.call-start = ((), (), s32[]{:S(2)}) async-start(), calls=%async_computation.8 | async-start | bytes 3981312 | tf_op jit(solution)/shard_map/all_gather | solution.py:793
  11.9 83.2 %all-gather.15.cloned.1.call-start = ((), (), s32[]{:S(2)}) async-start(), calls=%async_computation.9 | async-start | bytes 6635520 | tf_op jit(solution)/shard_map/all_gather | solution.py:799
  42.8 100.7 %all-gather.17.cloned.1.call-start = ((), (), s32[]{:S(2)}) async-start(), calls=%async_computation.10 | async-start | bytes 5308416 | tf_op jit(solution)/shard_map/all_gather | solution.py:800
  69.6 265.2 %all-gather.9.cloned.1.call-start = ((), (), s32[]{:S(2)}) async-start(), calls=%async_computation.4 | async-start | bytes 21233664 | tf_op jit(solution)/shard_map/all_gather | solution.py:803
  70.2 307.9 %all-gather.11.cloned.1.call-start = ((), (), s32[]{:S(2)}) async-start(), calls=%async_computation.5 | async-start | bytes 31850496 | tf_op jit(solution)/shard_map/all_gather | solution.py:803
  70.8 560.5 %reduce-scatter.9.cloned.1.call-start = ((), (), s32[]{:S(2)}) async-start(), calls=%async_computation.6 | async-start | bytes 21233664 | tf_op jit(solution)/shard_map/reduce_scatter | solution.py:1035
  79.1 42.7 %collective-permute-start.9 = (bf16[512,1536]{1,0:T(8,128)(2,1)S(1)}, bf16[512,1536]{1,0:T(8,128)(2,1)S(1)}, u32[]{:S(2)}, u32[]{:S(2)}) collective-permute-start(bf16[512,1536]{1,0:T(8,128)(2,1)S(1)} %copy-done.43), channel_id=1, source_target_pairs={{1,0},{2,1},{3,2},{5,4},{6,5},{7,6},{9,8},{10,9},{11,10},{13,12},{... | collective-permute-start | bytes 4718600 | tf_op jit(solution)/shard_map/ppermute | solution.py:632
  80.3 43.7 %collective-permute-start.7 = (bf16[512,1536]{1,0:T(8,128)(2,1)S(1)}, bf16[512,1536]{1,0:T(8,128)(2,1)}, u32[]{:S(2)}, u32[]{:S(2)}) collective-permute-start(bf16[512,1536]{1,0:T(8,128)(2,1)S(1)} %copy-done.43), channel_id=1, source_target_pairs={{0,1},{1,2},{2,3},{4,5},{5,6},{6,7},{8,9},{9,10},{10,11},{12,13},{... | collective-permute-start | bytes 4718600 | tf_op jit(solution)/shard_map/ppermute | solution.py:631
  121.7 37.6 %collective-permute-start.10 = (bf16[512,1536]{1,0:T(8,128)(2,1)S(1)}, bf16[512,1536]{1,0:T(8,128)(2,1)}, u32[]{:S(2)}, u32[]{:S(2)}) collective-permute-start(bf16[512,1536]{1,0:T(8,128)(2,1)S(1)} %collective-permute-done.9.refs_6_), channel_id=1, source_target_pairs={{1,0},{2,1},{5,4},{6,5},{9,8},{10,9},{13,12},{14,13},{17,16},{18,1... | collective-permute-start | bytes 4718600 | tf_op jit(solution)/shard_map/ppermute | solution.py:632
  213.3 57.1 %collective-permute-start.19 = (bf16[256,1536]{1,0:T(8,128)(2,1)}, bf16[256,1536]{1,0:T(8,128)(2,1)}, u32[]{:S(2)}, u32[]{:S(2)}) collective-permute-start(bf16[256,1536]{1,0:T(8,128)(2,1)} %collective-permute-done.18.refs_11_), channel_id=1, source_target_pairs={{2,3},{6,7},{10,11},{14,15},{18,19},{22,23},{26,27},{30,31}} | collective-permute-start | bytes 2359304 | tf_op jit(solution)/shard_map/ppermute | solution.py:631
  228.4 41.9 %collective-permute-start.22 = (bf16[256,1536]{1,0:T(8,128)(2,1)}, bf16[256,1536]{1,0:T(8,128)(2,1)}, u32[]{:S(2)}, u32[]{:S(2)}) collective-permute-start(bf16[256,1536]{1,0:T(8,128)(2,1)} %collective-permute-done.21.refs_14_), channel_id=1, source_target_pairs={{1,0},{5,4},{9,8},{13,12},{17,16},{21,20},{25,24},{29,28}} | collective-permute-start | bytes 2359304 | tf_op jit(solution)/shard_map/ppermute | solution.py:632
  229.7 40.6 %collective-permute-start.13 = (bf16[256,1536]{1,0:T(8,128)(2,1)}, bf16[256,1536]{1,0:T(8,128)(2,1)}, u32[]{:S(2)}, u32[]{:S(2)}) collective-permute-start(bf16[256,1536]{1,0:T(8,128)(2,1)} %collective-permute-done.12.refs_4_), channel_id=1, source_target_pairs={{2,3},{6,7},{10,11},{14,15},{18,19},{22,23},{26,27},{30,31}} | collective-permute-start | bytes 2359304 | tf_op jit(solution)/shard_map/ppermute | solution.py:631
  370.1 328.4 %reduce-scatter.13.cloned.1.call-start = ((), (), s32[]{:S(2)}) async-start(), calls=%async_computation.11 | async-start | bytes 17694720
  475.6 281.3 %reduce-scatter.11.cloned.1.call-start = ((), (), s32[]{:S(2)}) async-start(), calls=%async_computation.7 | async-start | bytes 7077888 | tf_op jit(solution)/shard_map/reduce_scatter | solution.py:1165
  525.6 61.1 %collective-permute-start.37 = (bf16[256,1664]{1,0:T(8,128)(2,1)S(1)}, bf16[256,1664]{1,0:T(8,128)(2,1)}, u32[]{:S(2)}, u32[]{:S(2)}) collective-permute-start(bf16[256,1664]{1,0:T(8,128)(2,1)S(1)} %add_convert_fusion.5), channel_id=1, source_target_pairs={{3,2},{2,1},{1,0},{7,6},{6,5},{5,4},{11,10},{10,9},{9,8},{15,14},{... | collective-permute-start | bytes 2555912 | tf_op jit(solution)/shard_map/ppermute | solution.py:652
  538.3 53.4 %collective-permute-start.36 = (bf16[256,1664]{1,0:T(8,128)(2,1)S(1)}, bf16[256,1664]{1,0:T(8,128)(2,1)}, u32[]{:S(2)}, u32[]{:S(2)}) collective-permute-start(bf16[256,1664]{1,0:T(8,128)(2,1)S(1)} %add_convert_fusion.6), channel_id=1, source_target_pairs={{0,1},{1,2},{2,3},{4,5},{5,6},{6,7},{8,9},{9,10},{10,11},{12,13},{... | collective-permute-start | bytes 2555912 | tf_op jit(solution)/shard_map/ppermute | solution.py:651
  556.6 40.0 %collective-permute-start.35 = (bf16[256,1664]{1,0:T(8,128)(2,1)S(1)}, bf16[256,1664]{1,0:T(8,128)(2,1)}, u32[]{:S(2)}, u32[]{:S(2)}) collective-permute-start(bf16[256,1664]{1,0:T(8,128)(2,1)S(1)} %add_convert_fusion.7), channel_id=1, source_target_pairs={{3,2},{2,1},{1,0},{7,6},{6,5},{5,4},{11,10},{10,9},{9,8},{15,14},{... | collective-permute-start | bytes 2555912 | tf_op jit(solution)/shard_map/ppermute | solution.py:652
  558.1 38.4 %collective-permute-start.34 = (bf16[256,1664]{1,0:T(8,128)(2,1)S(1)}, bf16[256,1664]{1,0:T(8,128)(2,1)}, u32[]{:S(2)}, u32[]{:S(2)}) collective-permute-start(bf16[256,1664]{1,0:T(8,128)(2,1)S(1)} %add_convert_fusion.8), channel_id=1, source_target_pairs={{0,1},{1,2},{2,3},{4,5},{5,6},{6,7},{8,9},{9,10},{10,11},{12,13},{... | collective-permute-start | bytes 2555912 | tf_op jit(solution)/shard_map/ppermute | solution.py:651
  584.9 67.4 %collective-permute-start.42 = (bf16[512,1536]{1,0:T(8,128)(2,1)}, bf16[512,1536]{1,0:T(8,128)(2,1)}, u32[]{:S(2)}, u32[]{:S(2)}) collective-permute-start(bf16[512,1536]{1,0:T(8,128)(2,1)} %get-tuple-element.125), channel_id=1, source_target_pairs={{3,2},{7,6},{11,10},{15,14},{19,18},{23,22},{27,26},{31,30}} | collective-permute-start | bytes 4718600 | tf_op jit(solution)/shard_map/ppermute | solution.py:652
  586.7 65.6 %collective-permute-start.33 = (bf16[512,1536]{1,0:T(8,128)(2,1)}, bf16[512,1536]{1,0:T(8,128)(2,1)}, u32[]{:S(2)}, u32[]{:S(2)}) collective-permute-start(bf16[512,1536]{1,0:T(8,128)(2,1)} %get-tuple-element.127), channel_id=1, source_target_pairs={{0,1},{4,5},{8,9},{12,13},{16,17},{20,21},{24,25},{28,29}} | collective-permute-start | bytes 4718600 | tf_op jit(solution)/shard_map/ppermute | solution.py:651
  631.3 132.3 %reduce-scatter.15.cloned.1.call-start = ((), (), s32[]{:S(2)}) async-start(), calls=%async_computation.12 | async-start | bytes 4915200
  657.1 36.7 %collective-permute-start.39 = (bf16[512,1536]{1,0:T(8,128)(2,1)}, bf16[512,1536]{1,0:T(8,128)(2,1)S(1)}, u32[]{:S(2)}, u32[]{:S(2)}) collective-permute-start(bf16[512,1536]{1,0:T(8,128)(2,1)} %get-tuple-element.220), channel_id=1, source_target_pairs={{0,1},{1,2},{4,5},{5,6},{8,9},{9,10},{12,13},{13,14},{16,17},{17,1... | collective-permute-start | bytes 4718600 | tf_op jit(solution)/shard_map/ppermute | solution.py:651
  707.6 40.6 %collective-permute-start.40 = (bf16[512,1536]{1,0:T(8,128)(2,1)}, bf16[512,1536]{1,0:T(8,128)(2,1)S(1)}, u32[]{:S(2)}, u32[]{:S(2)}) collective-permute-start(bf16[512,1536]{1,0:T(8,128)(2,1)} %add_convert_fusion.4), channel_id=1, source_target_pairs={{0,1},{1,2},{2,3},{4,5},{5,6},{6,7},{8,9},{9,10},{10,11},{12,13},{... | collective-permute-start | bytes 4718600 | tf_op jit(solution)/shard_map/ppermute | solution.py:651
  714.1 38.3 %collective-permute-start.44 = (bf16[512,1536]{1,0:T(8,128)(2,1)}, bf16[512,1536]{1,0:T(8,128)(2,1)S(1)}, u32[]{:S(2)}, u32[]{:S(2)}) collective-permute-start(bf16[512,1536]{1,0:T(8,128)(2,1)} %add_convert_fusion.3), channel_id=1, source_target_pairs={{3,2},{2,1},{1,0},{7,6},{6,5},{5,4},{11,10},{10,9},{9,8},{15,14},{... | collective-permute-start | bytes 4718600 | tf_op jit(solution)/shard_map/ppermute | solution.py:652
  (92 other events, 1818.4 us)
Sparse Core Ops, SparseCore 0:
  12.0 36.6 all-gather.12
  51.2 43.8 all-gather.14
  97.0 38.9 all-gather.16
  138.3 98.7 all-gather.8
  239.4 138.6 all-gather.10
  381.5 126.1 reduce-scatter.8
  510.8 133.6 reduce-scatter.12
  647.9 61.7 reduce-scatter.10
  713.0 50.6 reduce-scatter.14

commit v2 on v1

--- a/solution.py
+++ b/solution.py
@@ -1146,8 +1146,6 @@
         in_grad.append(part[..., : 2 * FF].astype(F32))
         down_grad.append(part[..., 2 * FF :].astype(F32))
     in_grad, down_grad = jnp.concatenate(in_grad), jnp.concatenate(down_grad)
-    last = tuple(after(part, in_grad, down_grad) for part in combined_steps[-1])
-    layer_out = (middle + summed(combined, [last])).astype(BF16)
     input_grad, attn_gain_grad = pl.pallas_call(
         input_back_kernel,
         grid=(rows // LANES,),
@@ -1162,35 +1160,38 @@
         name="input_back",
     )(tokens, normed_one_grad, attn_gain[None, :], jnp.concatenate(middle_grads))
 
-    second_sum = lax.psum_scatter(
-        after(second_term, weight_sums[0]), "gx", scatter_dimension=0, tiled=True
-    )
-    second_sum = lax.optimization_barrier(second_sum)[0]
-    mine, other = joined_terms
-    other = after(other, combined_steps[1], attn_gain_grad)
-    joined_sum = pair_scatter(mine, other, nx, second_sum, *added, *weight_sums)
-    gain_sums = after(jnp.concatenate([attn_gain_grad, moe_gain_grad]), layer_out)
+    gain_sums = jnp.concatenate([attn_gain_grad, moe_gain_grad])
     bit = 1
     while bit < nx:
         pairs = [(s, s ^ bit) for s in range(nx)]
         gain_sums = gain_sums + lax.ppermute(gain_sums, "gx", pairs)
         bit = 2 * bit
+    last = tuple(after(part, in_grad, down_grad, gain_sums) for part in combined_steps[-1])
+    layer_out = (middle + summed(combined, [last])).astype(BF16)
+
+    second_sum = lax.psum_scatter(
+        after(second_term, weight_sums[0]), "gx", scatter_dimension=0, tiled=True
+    )
+    second_sum = lax.optimization_barrier(second_sum)[0]
+    mine, other = joined_terms
+    other = after(other, combined_steps[1], attn_gain_grad)
+    joined_sum = pair_scatter(mine, other, nx, second_sum, *added, *weight_sums)
     high = gain_sums.astype(BF16)
     low = (gain_sums - high.astype(F32)).astype(BF16)
     gains = jnp.stack([high, low]).reshape(-1)
     gain_rows = -(-gains.shape[0] // joined)
     gain_rows += -gain_rows % SUBLANES
     gains = jnp.pad(gains, (0, gain_rows * joined - gains.shape[0])).reshape(gain_rows, joined)
-    joined_sum = after(joined_sum, gains)
+    second_sum = direct_sum(second_sum, ny, layer_out)
+    out_weight_grad = second_sum[:, :heads_width].T
+    router_grad = second_sum[:, width : width + experts].T
+    joined_sum = after(joined_sum, gains, out_weight_grad, router_grad)
     joined_parts, gain_parts = [joined_sum[0]], [gains]
     for k in range(1, ny):
         part = jnp.concatenate([joined_sum[k], gains], axis=0)
         part = lax.ppermute(part, "gy", [(s, (s - k) % ny) for s in range(ny)])
         joined_parts.append(part)
         gain_parts.append(part[depth:])
-    second_sum = direct_sum(second_sum, ny, *joined_parts[1:])
-    out_weight_grad = second_sum[:, :heads_width].T
-    router_grad = second_sum[:, width : width + experts].T
     qkv_grad = pl.pallas_call(
         functools.partial(joined_sum_kernel, groups),
         out_shape=jax.ShapeDtypeStruct(query_key_value_weight.shape, F32),

time: 827 us -> 819 us (level)
  waiting for transfers between devices: 233 us -> 220 us
    ppermute x3, waiting for transfers between devices: 28 us -> 18.5 us  [shards(): part = lax.ppermute(part, 'gy', [(s, (s - k) % ny) for s in range(ny)])]
  transfers between devices with their start and end apart: 64 -> 64, of which waited for: 32 -> 30; matrix products, arithmetic and copies ran while one was open for 13% -> 13% of each run, Pallas kernels for 38% -> 38%
where the time goes in v2:
time: 819 us; the launch traced here: 810 us
  Pallas kernels  314 us (38%)
  waiting for transfers between devices  220 us (27%)
  starting transfers between devices  136 us (17%)
  other arithmetic  81.6 us (10%)
  local copies, waits for them, and re-layouts  42.6 us (5%)
  between operations  15.5 us (2%)
    pallas_call x2, Pallas kernels, shards(): pl.pallas_call(functools.partial(expert_kernel, lo, experts), grid=(hi -...  89.4 us
    ppermute x9, waiting for transfers between devices, gather_step(): lax.ppermute(down, 'gy', [(s + 1, s) for s in range(0, size - 1 - step)])  56.4 us
    ppermute x9, waiting for transfers between devices, sum_sent(): lax.ppermute(above, 'gy', [(s, s + 1) for s in range(step)])  54.8 us
    pallas_call x2, Pallas kernels, combine(): pl.pallas_call(functools.partial(combine_kernel, more, tuple((hi - lo for...  44.8 us
    ppermute x9, starting transfers between devices, sum_sent(): lax.ppermute(above, 'gy', [(s, s + 1) for s in range(step)])  43.2 us
    pallas_call x2, Pallas kernels, shards(): pl.pallas_call(attend_back_kernel, grid=(ny,), in_specs=[half_rows(n, wid...  38.5 us
    ppermute x9, starting transfers between devices, gather_step(): lax.ppermute(up, 'gy', [(s, s + 1) for s in range(step, size - 1)])  37.2 us
    ppermute x6, waiting for transfers between devices, direct_gather(): lax.ppermute(part, 'gy', [(s, (s + k) % size) for s in range(size)])  29.7 us
  transfers between devices with their start and end apart: 64, of which 30 were waited for; matrix products, arithmetic and copies ran while one was open for 13% of the time, Pallas kernels for 38%

profile of v2, /device:TPU:0, one launch (start us, length us, event | category | flops | bytes accessed | tf_op | source)
XLA Modules:
  0.0 809.6 jit_solution(14138185590946361807)
XLA Ops:
  26.8 13.2 %collective-permute-done.1 = bf16[192,640]{0,1:T(8,128)(2,1)} collective-permute-done((bf16[192,640]{0,1:T(8,128)(2,1)}, bf16[192,640]{0,1:T(8,128)(2,1)}, u32[]{:S(2)}, u32[]{:S(2)}) %collective-permute-start.1) | collective-permute-done | bytes 245792 | tf_op jit(solution)/shard_map/ppermute | solution.py:622
  58.9 9.4 %collective-permute-done.5 = bf16[192,512]{0,1:T(8,128)(2,1)S(1)} collective-permute-done((bf16[192,512]{0,1:T(8,128)(2,1)S(1)}, bf16[192,512]{0,1:T(8,128)(2,1)S(1)}, u32[]{:S(2)}, u32[]{:S(2)}) %collective-permute-start.5) | collective-permute-done | bytes 196640 | tf_op jit(solution)/shard_map/ppermute | solution.py:622
  80.3 10.0 %collective-permute-start.7 = (bf16[512,1536]{1,0:T(8,128)(2,1)S(1)}, bf16[512,1536]{1,0:T(8,128)(2,1)}, u32[]{:S(2)}, u32[]{:S(2)}) collective-permute-start(bf16[512,1536]{1,0:T(8,128)(2,1)S(1)} %copy-done.45), channel_id=1, source_target_pairs={{0,1},{1,2},{2,3},{4,5},{5,6},{6,7},{8,9},{9,10},{10,11},{12,13},{... | collective-permute-start | bytes 4718600 | tf_op jit(solution)/shard_map/ppermute | solution.py:631
  95.1 11.2 %project.1 = (bf16[512,1536]{1,0:T(8,128)(2,1)}, bf16[512,1024]{1,0:T(8,128)(2,1)}) custom-call(bf16[512,1536]{1,0:T(8,128)(2,1)} %copy.95.normed_ref, bf16[8,192,1152]{2,1,0:T(8,128)(2,1)} %bitcast.113, bf16[8,3,192,640]{3,2,1,0:T(8,128)(2,1)} %bitcast.121, f32[512,128]{1,0:T(8,128)} %get-tuple-element.247.cos_ref.refs_10_, ...), custom_call_target="tpu_custom_call" | custom-call | flops 11000000512 | bytes 36000000 | tf_op jit(solution)/shard_map/project/pallas_call | solution.py:818
  143.5 9.5 %branch.1 = (f32[512,1536]{1,0:T(8,128)}, bf16[256,1536]{1,0:T(8,128)(2,1)}, bf16[256,1536]{1,0:T(8,128)(2,1)}) custom-call(bf16[256,1536]{1,0:T(8,128)(2,1)} %attend.2.refs_0_.refs_6_, bf16[256,1536]{1,0:T(8,128)(2,1)} %attend.3.refs_1_.refs_7_, bf16[8,192,1152]{2,1,0:T(8,128)(2,1)} %bitcast.114, bf16[8,3,192,512]{3,2,1,0:T(8,128)(2,1)} %bitcast.102, ...), custom_call_target="tpu_custom_call" | custom-call | flops 7699999744 | bytes 25200000 | tf_op jit(solution)/shard_map/branch/pallas_call | solution.py:867
  159.3 12.3 %collective-permute-start.17 = (bf16[256,1536]{1,0:T(8,128)(2,1)}, bf16[256,1536]{1,0:T(8,128)(2,1)S(1)}, u32[]{:S(2)}, u32[]{:S(2)}) collective-permute-start(bf16[256,1536]{1,0:T(8,128)(2,1)} %get-tuple-element.104.refs_9_), channel_id=1, source_target_pairs={{0,1},{1,2},{2,3},{4,5},{5,6},{6,7},{8,9},{9,10},{10,11},{12,13},{... | collective-permute-start | bytes 2359304 | tf_op jit(solution)/shard_map/ppermute | solution.py:631
  180.1 9.8 %collective-permute-done.17.refs_10_ = bf16[256,1536]{1,0:T(8,128)(2,1)S(1)} collective-permute-done((bf16[256,1536]{1,0:T(8,128)(2,1)}, bf16[256,1536]{1,0:T(8,128)(2,1)S(1)}, u32[]{:S(2)}, u32[]{:S(2)}) %collective-permute-start.17) | collective-permute-done | bytes 786464 | tf_op jit(solution)/shard_map/ppermute | solution.py:631
  214.8 13.6 %collective-permute-done.21.refs_14_ = bf16[256,1536]{1,0:T(8,128)(2,1)} collective-permute-done((bf16[256,1536]{1,0:T(8,128)(2,1)S(1)}, bf16[256,1536]{1,0:T(8,128)(2,1)}, u32[]{:S(2)}, u32[]{:S(2)}) %collective-permute-start.21) | collective-permute-done | bytes 786464 | tf_op jit(solution)/shard_map/ppermute | solution.py:632
  231.3 14.0 %collective-permute-done.15.refs_7_ = bf16[256,1536]{1,0:T(8,128)(2,1)} collective-permute-done((bf16[256,1536]{1,0:T(8,128)(2,1)}, bf16[256,1536]{1,0:T(8,128)(2,1)}, u32[]{:S(2)}, u32[]{:S(2)}) %collective-permute-start.15) | collective-permute-done | bytes 786464 | tf_op jit(solution)/shard_map/ppermute | solution.py:632
  246.6 11.5 %compare_reduce_fusion = pred[2048,128]{1,0:T(8,128)(4,1)S(1)} fusion(s32[128]{0:T(128)S(1)} %compare_select_fusion.5, s32[2048,8]{1,0:T(8,128)S(1)} %copy.102), kind=kLoop, calls=%fused_computation.2 | loop fusion | flops 3932160 | bytes 328192 | tf_op jit(solution)/shard_map/reduce_or | solution.py:744
  278.7 27.4 %dispatch_rows.1 = (bf16[10,464,1536]{2,1,0:T(8,128)(2,1)}, f32[10,464,128]{2,1,0:T(8,128)}) custom-call(s32[4]{0:T(128)} %and_select_fusion.6.refs_0_, s32[16,9]{1,0:T(8,128)} %bitcast.123, bf16[256,1536]{1,0:T(8,128)(2,1)} %get-tuple-element.102.refs_2_, bf16[256,1536]{1,0:T(8,128)(2,1)} %collective-permute-done.11.refs_3_, ...), custom_call_target="tpu_custom_call" | custom-call | flops 34100000768 | bytes 111600000 | tf_op jit(solution)/shard_map/dispatch_rows/pallas_call | solution.py:929
  315.0 19.7 %dispatch_grads.1.grad_ref = bf16[10,464,1536]{2,1,0:T(8,128)(2,1)} custom-call(s32[4]{0:T(128)} %and_select_fusion.6.refs_0_, s32[16,9]{1,0:T(8,128)} %bitcast.124, bf16[512,1536]{1,0:T(8,128)(2,1)} %grad_ref.3, bf16[512,1536]{1,0:T(8,128)(2,1)} %collective-permute-done.7.refs_3_, bf16[512,1536]{1,0:T(8,128)(2,1)} %collective-permute-done.8.refs_4_, ...), custom_call_target="tpu_custom_call" | custom-call | flops 28600000512 | bytes 93600000 | tf_op jit(solution)/shard_map/dispatch_grads/pallas_call | solution.py:919
  334.8 35.2 %experts.2 = (bf16[4,464,1536]{2,1,0:T(8,128)(2,1)}, bf16[4,464,1536]{2,1,0:T(8,128)(2,1)}, bf16[4,464,128]{2,1,0:T(8,128)(2,1)}, bf16[8,4,192,1536]{3,2,1,0:T(8,128)(2,1)}) custom-call(s32[1]{0:T(128)} %bitcast.20.half_ref.refs_6_, bf16[10,464,1536]{2,1,0:T(8,128)(2,1)} %get-tuple-element.105.x_ref, bf16[10,464,1536]{2,1,0:T(8,128)(2,1)} %dispatch_grads.1.grad_ref, ...), custom_call_target="tpu_custom_call" | custom-call | flops 39600001024 | bytes 129600000 | tf_op jit(solution)/shard_map/experts/pallas_call | solution.py:947
  378.0 54.2 %experts.3 = (bf16[6,464,1536]{2,1,0:T(8,128)(2,1)}, bf16[6,464,1536]{2,1,0:T(8,128)(2,1)}, bf16[6,464,128]{2,1,0:T(8,128)(2,1)}, bf16[4,6,192,1536]{3,2,1,0:T(8,128)(2,1)}, bf16[4,6,192,1536]{3,2,1,0:T(8,128)(2,1)}) custom-call(s32[1]{0:T(128)} %bitcast.20.half_ref.refs_6_, bf16[10,464,1536]{2,1,0:T(8,128)(2,1)} %get-tuple-element.105.x_ref, ...), custom_call_target="tpu_custom_call" | custom-call | flops 59399999488 | bytes 194400000 | tf_op jit(solution)/shard_map/experts/pallas_call | solution.py:947
  435.1 23.9 %combine_grads.1 = (bf16[256,1664]{1,0:T(8,128)(2,1)}, bf16[256,1664]{1,0:T(8,128)(2,1)}, bf16[256,1664]{1,0:T(8,128)(2,1)}, bf16[256,1664]{1,0:T(8,128)(2,1)}, ...) custom-call(s32[4]{0:T(128)} %gather_fusion, ...), custom_call_target="tpu_custom_call" | custom-call | flops 17600000000 | bytes 57600000 | tf_op jit(solution)/shard_map/combine_grads/pallas_call | solution.py:991
  459.0 16.4 %add_convert_fusion = bf16[4,6,192,1536]{3,2,1,0:T(8,128)(2,1)} fusion(bf16[4,6,192,1536]{3,2,1,0:T(8,128)(2,1)} %collective-permute-done.41, bf16[4,6,192,1536]{3,2,1,0:T(8,128)(2,1)} %get-tuple-element.137), kind=kLoop, calls=%fused_computation.1 | loop fusion | flops 28311552 | bytes 42467328 | tf_op jit(solution)/shard_map/convert_element_type | solution.py:613
  526.7 11.2 %collective-permute-done.30 = bf16[256,1664]{1,0:T(8,128)(2,1)S(1)} collective-permute-done((bf16[256,1664]{1,0:T(8,128)(2,1)S(1)}, bf16[256,1664]{1,0:T(8,128)(2,1)S(1)}, u32[]{:S(2)}, u32[]{:S(2)}) %collective-permute-start.30) | collective-permute-done | bytes 852000 | tf_op jit(solution)/shard_map/ppermute | solution.py:651
  543.4 12.8 %collective-permute-done.26 = bf16[256,1664]{1,0:T(8,128)(2,1)S(1)} collective-permute-done((bf16[256,1664]{1,0:T(8,128)(2,1)S(1)}, bf16[256,1664]{1,0:T(8,128)(2,1)S(1)}, u32[]{:S(2)}, u32[]{:S(2)}) %collective-permute-start.26) | collective-permute-done | bytes 852000 | tf_op jit(solution)/shard_map/ppermute | solution.py:651
  563.9 20.9 %combine_rows.1 = (bf16[512,1536]{1,0:T(8,128)(2,1)}, bf16[512,1536]{1,0:T(8,128)(2,1)}, bf16[512,1536]{1,0:T(8,128)(2,1)}, bf16[512,1536]{1,0:T(8,128)(2,1)}) custom-call(s32[4]{0:T(128)} %gather_fusion, s32[16,9]{1,0:T(8,128)} %bitcast.126, s32[2048,128]{1,0:T(8,128)} %pad.18.refs_2_, bf16[4,464,1536]{2,1,0:T(8,128)(2,1)} %get-tuple-element.120.refs_3_, ...), custom_call_target="tpu_custom_call" | custom-call | flops 17600000000 | bytes 57600000 | tf_op jit(solution)/shard_map/combine_rows/pallas_call | solution.py:991
  601.5 19.7 %attend_back.2 = (bf16[256,1536]{1,0:T(8,128)(2,1)}, f32[256,1024]{1,0:T(8,128)}, bf16[256,1024]{1,0:T(8,128)(2,1)}) custom-call(bf16[512,1536]{1,0:T(8,128)(2,1)} %get-tuple-element.92.query_ref, bf16[512,1024]{1,0:T(8,128)(2,1)} %get-tuple-element.93.own_ref.before_ref, bf16[256,1024]{1,0:T(8,128)(2,1)} %collective-permute-done.3.before_ref, ...), custom_call_target="tpu_custom_call" | custom-call | flops 18699999232 | bytes 61200000 | tf_op jit(solution)/shard_map/attend_back/pallas_call | solution.py:1074
  631.4 18.8 %attend_back.3 = (bf16[256,1536]{1,0:T(8,128)(2,1)}, f32[256,1024]{1,0:T(8,128)}, f32[256,1024]{1,0:T(8,128)}) custom-call(bf16[512,1536]{1,0:T(8,128)(2,1)} %get-tuple-element.92.query_ref, bf16[512,1024]{1,0:T(8,128)(2,1)} %get-tuple-element.93.own_ref.before_ref, bf16[512,1024]{1,0:T(8,128)(2,1)} %get-tuple-element.93.own_ref.before_ref, ...), custom_call_target="tpu_custom_call" | custom-call | flops 18699999232 | bytes 61200000 | tf_op jit(solution)/shard_map/attend_back/pallas_call | solution.py:1074
  663.6 24.4 %project_back.1 = (bf16[4,4,192,640]{3,2,1,0:T(8,128)(2,1)}, bf16[4,4,192,640]{3,2,1,0:T(8,128)(2,1)}, f32[512,1536]{1,0:T(8,128)}) custom-call(bf16[256,1536]{1,0:T(8,128)(2,1)} %get-tuple-element.140.refs_0_, bf16[256,1536]{1,0:T(8,128)(2,1)} %get-tuple-element.142.refs_1_, f32[256,1024]{1,0:T(8,128)} %get-tuple-element.143.refs_2_, ...), custom_call_target="tpu_custom_call" | custom-call | flops 24199999488 | bytes 79200000 | tf_op jit(solution)/shard_map/project_back/pallas_call | solution.py:1121
  740.2 15.5 %collective-permute-done.40 = bf16[512,1536]{1,0:T(8,128)(2,1)} collective-permute-done((bf16[512,1536]{1,0:T(8,128)(2,1)}, bf16[512,1536]{1,0:T(8,128)(2,1)}, u32[]{:S(2)}, u32[]{:S(2)}) %collective-permute-start.40) | collective-permute-done | bytes 1572896 | tf_op jit(solution)/shard_map/ppermute | solution.py:651
  786.6 13.0 %collective-permute-done.53.refs_2_ = bf16[208,640]{1,0:T(8,128)(2,1)S(1)} collective-permute-done((bf16[208,640]{1,0:T(8,128)(2,1)S(1)}, bf16[208,640]{1,0:T(8,128)(2,1)S(1)}, u32[]{:S(2)}, u32[]{:S(2)}) %collective-permute-start.53) | collective-permute-done | bytes 266272 | tf_op jit(solution)/shard_map/ppermute | solution.py:1192
  (362 shorter events, 366.4 us)
Async XLA Ops:
  7.2 83.2 %all-gather.13.cloned.1.call-start = ((), (), s32[]{:S(2)}) async-start(), calls=%async_computation.8 | async-start | bytes 3981312 | tf_op jit(solution)/shard_map/all_gather | solution.py:793
  11.9 83.2 %all-gather.15.cloned.1.call-start = ((), (), s32[]{:S(2)}) async-start(), calls=%async_computation.9 | async-start | bytes 6635520 | tf_op jit(solution)/shard_map/all_gather | solution.py:799
  42.8 100.7 %all-gather.17.cloned.1.call-start = ((), (), s32[]{:S(2)}) async-start(), calls=%async_computation.10 | async-start | bytes 5308416 | tf_op jit(solution)/shard_map/all_gather | solution.py:800
  69.6 265.2 %all-gather.9.cloned.1.call-start = ((), (), s32[]{:S(2)}) async-start(), calls=%async_computation.4 | async-start | bytes 21233664 | tf_op jit(solution)/shard_map/all_gather | solution.py:803
  70.2 307.9 %all-gather.11.cloned.1.call-start = ((), (), s32[]{:S(2)}) async-start(), calls=%async_computation.5 | async-start | bytes 31850496 | tf_op jit(solution)/shard_map/all_gather | solution.py:803
  70.7 560.6 %reduce-scatter.9.cloned.1.call-start = ((), (), s32[]{:S(2)}) async-start(), calls=%async_computation.6 | async-start | bytes 21233664 | tf_op jit(solution)/shard_map/reduce_scatter | solution.py:1035
  79.0 42.6 %collective-permute-start.9 = (bf16[512,1536]{1,0:T(8,128)(2,1)S(1)}, bf16[512,1536]{1,0:T(8,128)(2,1)S(1)}, u32[]{:S(2)}, u32[]{:S(2)}) collective-permute-start(bf16[512,1536]{1,0:T(8,128)(2,1)S(1)} %copy-done.45), channel_id=1, source_target_pairs={{1,0},{2,1},{3,2},{5,4},{6,5},{7,6},{9,8},{10,9},{11,10},{13,12},{... | collective-permute-start | bytes 4718600 | tf_op jit(solution)/shard_map/ppermute | solution.py:632
  80.3 43.7 %collective-permute-start.7 = (bf16[512,1536]{1,0:T(8,128)(2,1)S(1)}, bf16[512,1536]{1,0:T(8,128)(2,1)}, u32[]{:S(2)}, u32[]{:S(2)}) collective-permute-start(bf16[512,1536]{1,0:T(8,128)(2,1)S(1)} %copy-done.45), channel_id=1, source_target_pairs={{0,1},{1,2},{2,3},{4,5},{5,6},{6,7},{8,9},{9,10},{10,11},{12,13},{... | collective-permute-start | bytes 4718600 | tf_op jit(solution)/shard_map/ppermute | solution.py:631
  213.2 57.0 %collective-permute-start.19 = (bf16[256,1536]{1,0:T(8,128)(2,1)}, bf16[256,1536]{1,0:T(8,128)(2,1)}, u32[]{:S(2)}, u32[]{:S(2)}) collective-permute-start(bf16[256,1536]{1,0:T(8,128)(2,1)} %collective-permute-done.18.refs_11_), channel_id=1, source_target_pairs={{2,3},{6,7},{10,11},{14,15},{18,19},{22,23},{26,27},{30,31}} | collective-permute-start | bytes 2359304 | tf_op jit(solution)/shard_map/ppermute | solution.py:631
  228.4 41.8 %collective-permute-start.22 = (bf16[256,1536]{1,0:T(8,128)(2,1)}, bf16[256,1536]{1,0:T(8,128)(2,1)}, u32[]{:S(2)}, u32[]{:S(2)}) collective-permute-start(bf16[256,1536]{1,0:T(8,128)(2,1)} %collective-permute-done.21.refs_14_), channel_id=1, source_target_pairs={{1,0},{5,4},{9,8},{13,12},{17,16},{21,20},{25,24},{29,28}} | collective-permute-start | bytes 2359304 | tf_op jit(solution)/shard_map/ppermute | solution.py:632
  229.7 40.5 %collective-permute-start.13 = (bf16[256,1536]{1,0:T(8,128)(2,1)}, bf16[256,1536]{1,0:T(8,128)(2,1)}, u32[]{:S(2)}, u32[]{:S(2)}) collective-permute-start(bf16[256,1536]{1,0:T(8,128)(2,1)} %collective-permute-done.12.refs_4_), channel_id=1, source_target_pairs={{2,3},{6,7},{10,11},{14,15},{18,19},{22,23},{26,27},{30,31}} | collective-permute-start | bytes 2359304 | tf_op jit(solution)/shard_map/ppermute | solution.py:631
  370.0 328.8 %reduce-scatter.13.cloned.1.call-start = ((), (), s32[]{:S(2)}) async-start(), calls=%async_computation.11 | async-start | bytes 17694720
  475.5 250.8 %reduce-scatter.11.cloned.1.call-start = ((), (), s32[]{:S(2)}) async-start(), calls=%async_computation.7 | async-start | bytes 7077888 | tf_op jit(solution)/shard_map/reduce_scatter | solution.py:1172
  525.4 61.1 %collective-permute-start.37 = (bf16[256,1664]{1,0:T(8,128)(2,1)S(1)}, bf16[256,1664]{1,0:T(8,128)(2,1)}, u32[]{:S(2)}, u32[]{:S(2)}) collective-permute-start(bf16[256,1664]{1,0:T(8,128)(2,1)S(1)} %add_convert_fusion.5), channel_id=1, source_target_pairs={{3,2},{2,1},{1,0},{7,6},{6,5},{5,4},{11,10},{10,9},{9,8},{15,14},{... | collective-permute-start | bytes 2555912 | tf_op jit(solution)/shard_map/ppermute | solution.py:652
  538.1 53.7 %collective-permute-start.36 = (bf16[256,1664]{1,0:T(8,128)(2,1)S(1)}, bf16[256,1664]{1,0:T(8,128)(2,1)}, u32[]{:S(2)}, u32[]{:S(2)}) collective-permute-start(bf16[256,1664]{1,0:T(8,128)(2,1)S(1)} %add_convert_fusion.6), channel_id=1, source_target_pairs={{0,1},{1,2},{2,3},{4,5},{5,6},{6,7},{8,9},{9,10},{10,11},{12,13},{... | collective-permute-start | bytes 2555912 | tf_op jit(solution)/shard_map/ppermute | solution.py:651
  556.4 40.3 %collective-permute-start.35 = (bf16[256,1664]{1,0:T(8,128)(2,1)S(1)}, bf16[256,1664]{1,0:T(8,128)(2,1)}, u32[]{:S(2)}, u32[]{:S(2)}) collective-permute-start(bf16[256,1664]{1,0:T(8,128)(2,1)S(1)} %add_convert_fusion.7), channel_id=1, source_target_pairs={{3,2},{2,1},{1,0},{7,6},{6,5},{5,4},{11,10},{10,9},{9,8},{15,14},{... | collective-permute-start | bytes 2555912 | tf_op jit(solution)/shard_map/ppermute | solution.py:652
  558.0 38.8 %collective-permute-start.34 = (bf16[256,1664]{1,0:T(8,128)(2,1)S(1)}, bf16[256,1664]{1,0:T(8,128)(2,1)}, u32[]{:S(2)}, u32[]{:S(2)}) collective-permute-start(bf16[256,1664]{1,0:T(8,128)(2,1)S(1)} %add_convert_fusion.8), channel_id=1, source_target_pairs={{0,1},{1,2},{2,3},{4,5},{5,6},{6,7},{8,9},{9,10},{10,11},{12,13},{... | collective-permute-start | bytes 2555912 | tf_op jit(solution)/shard_map/ppermute | solution.py:651
  584.7 67.4 %collective-permute-start.45 = (bf16[512,1536]{1,0:T(8,128)(2,1)}, bf16[512,1536]{1,0:T(8,128)(2,1)}, u32[]{:S(2)}, u32[]{:S(2)}) collective-permute-start(bf16[512,1536]{1,0:T(8,128)(2,1)} %get-tuple-element.124), channel_id=1, source_target_pairs={{3,2},{7,6},{11,10},{15,14},{19,18},{23,22},{27,26},{31,30}} | collective-permute-start | bytes 4718600 | tf_op jit(solution)/shard_map/ppermute | solution.py:652
  586.6 65.6 %collective-permute-start.33 = (bf16[512,1536]{1,0:T(8,128)(2,1)}, bf16[512,1536]{1,0:T(8,128)(2,1)}, u32[]{:S(2)}, u32[]{:S(2)}) collective-permute-start(bf16[512,1536]{1,0:T(8,128)(2,1)} %get-tuple-element.126), channel_id=1, source_target_pairs={{0,1},{4,5},{8,9},{12,13},{16,17},{20,21},{24,25},{28,29}} | collective-permute-start | bytes 4718600 | tf_op jit(solution)/shard_map/ppermute | solution.py:651
  631.4 144.7 %reduce-scatter.15.cloned.1.call-start = ((), (), s32[]{:S(2)}) async-start(), calls=%async_computation.12 | async-start | bytes 4915200
  714.9 40.8 %collective-permute-start.40 = (bf16[512,1536]{1,0:T(8,128)(2,1)}, bf16[512,1536]{1,0:T(8,128)(2,1)}, u32[]{:S(2)}, u32[]{:S(2)}) collective-permute-start(bf16[512,1536]{1,0:T(8,128)(2,1)} %add_convert_fusion.4), channel_id=1, source_target_pairs={{0,1},{1,2},{2,3},{4,5},{5,6},{6,7},{8,9},{9,10},{10,11},{12,13},{... | collective-permute-start | bytes 4718600 | tf_op jit(solution)/shard_map/ppermute | solution.py:651
  721.7 39.4 %collective-permute-start.47 = (bf16[512,1536]{1,0:T(8,128)(2,1)}, bf16[512,1536]{1,0:T(8,128)(2,1)}, u32[]{:S(2)}, u32[]{:S(2)}) collective-permute-start(bf16[512,1536]{1,0:T(8,128)(2,1)} %add_convert_fusion.3), channel_id=1, source_target_pairs={{3,2},{2,1},{1,0},{7,6},{6,5},{5,4},{11,10},{10,9},{9,8},{15,14},{... | collective-permute-start | bytes 4718600 | tf_op jit(solution)/shard_map/ppermute | solution.py:652
  728.9 45.4 %collective-permute-start.50 = (bf16[192,512]{1,0:T(8,128)(2,1)S(1)}, bf16[192,512]{1,0:T(8,128)(2,1)S(1)}, u32[]{:S(2)}, u32[]{:S(2)}) collective-permute-start(bf16[192,512]{1,0:T(8,128)(2,1)S(1)} %get-tuple-element.232), channel_id=1, source_target_pairs={{0,2},{1,3},{2,0},{3,1},{4,6},{5,7},{6,4},{7,5},{8,10},{9,11},{10,... | collective-permute-start | bytes 589832 | tf_op jit(solution)/shard_map/ppermute | solution.py:670
  731.7 42.6 %collective-permute-start.51 = (bf16[192,512]{1,0:T(8,128)(2,1)S(1)}, bf16[192,512]{1,0:T(8,128)(2,1)S(1)}, u32[]{:S(2)}, u32[]{:S(2)}) collective-permute-start(bf16[192,512]{1,0:T(8,128)(2,1)S(1)} %get-tuple-element.231), channel_id=1, source_target_pairs={{0,1},{1,2},{2,3},{3,0},{4,5},{5,6},{6,7},{7,4},{8,9},{9,10},{10,1... | collective-permute-start | bytes 589832 | tf_op jit(solution)/shard_map/ppermute | solution.py:670
  (94 other events, 1807.7 us)
Sparse Core Ops, SparseCore 0:
  12.0 36.6 all-gather.12
  51.2 43.8 all-gather.14
  97.0 38.9 all-gather.16
  138.3 98.7 all-gather.8
  239.4 138.6 all-gather.10
  381.5 126.1 reduce-scatter.8
  510.8 133.5 reduce-scatter.12
  648.4 61.7 reduce-scatter.10
  713.5 50.4 reduce-scatter.14
